TPU v7x, 128 devices: a whole 4x4x4 slice. The times are simulated.
128 devices in a mesh: items: 32 (over z, x, core), book: 4 (over y).
Axes of the slice: x: 4, y: 4, z: 4, core: 2. Of those that a mesh axis runs over, the one named last changes fastest.
Arguments:
- hidden: bfloat16 [32768, 768], P(('items', 'book')), may hold values from -24 to 24
- enc_weight: bfloat16 [768, 768], replicated, may hold values from -0.21875 to 0.21875
- codebook: bfloat16 [3, 8192, 768], P(None, 'book'), may hold values from -4 to 4
- codes: int32 [3, 32768], P(None, ('items', 'book')), may hold values from 0 to 8191, as said below
Outputs:
- code_grad: float32 [3, 4, 2048, 768], P(None, 'book', 'items')
- enc_grad: float32 [768, 768], replicated
- last_residual: float32 [32768, 768], P(('items', 'book'))
Inputs may be any that keep to these rules, and one draw needn't show every extreme that they name: At every level, among the 256 items of one device (aligned blocks of 256 items) at most 128 have a code in any one block of 2048 consecutive codes, and in every block and level one such code block holds exactly 128 of them.
All inputs are finite; a program needn't handle non-finite values.
Results may differ from a plain program's by a relative error of at most 0.0019.
Values may be sent and summed in bfloat16 or wider, within the bound.
A program may use at most 128 MiB of HBM per device.

v0:
```python
import jax
import jax.numpy as jnp
from jax import lax
from jax.sharding import PartitionSpec as P


def own_rows(portion, extent, axis):
    count = extent * lax.axis_size(axis)
    return lax.psum_scatter(portion(jnp.int32(0), count), axis, scatter_dimension=0, tiled=True)


def code_hits(identities, offset, count):
    columns = jnp.arange(count, dtype=jnp.int32)
    return (identities[:, None] - offset == columns[None, :]).astype(jnp.bfloat16)


def on_device(hidden, enc_weight, codebook, codes):
    tok = hidden.shape[0]
    width = hidden.shape[1]
    levels = codebook.shape[0]
    shard_rows = codebook.shape[1]
    lifted = jnp.dot(hidden, enc_weight, preferred_element_type=jnp.float32)
    group_codes = lax.all_gather(codes, "book", axis=1, tiled=True)
    offset = lax.axis_index("book") * shard_rows
    columns = []
    for fetch_level in range(levels):
        identities = group_codes[fetch_level]
        hits = code_hits(identities, offset, shard_rows)
        columns.append(jnp.dot(hits, codebook[fetch_level], preferred_element_type=jnp.float32))
    fetched = lax.psum_scatter(
        jnp.concatenate(columns, axis=1).astype(jnp.bfloat16),
        "book",
        scatter_dimension=0,
        tiled=True,
    ).astype(jnp.float32)
    residual = lifted
    history = []
    for level in range(levels):
        residual = residual - fetched[:, level * width : (level + 1) * width]
        history.append(residual)
    carried = jnp.zeros(lifted.shape, jnp.float32)
    grads = [None] * levels
    for level in reversed(range(levels)):
        carried = carried + history[level]
        grads[level] = carried.astype(jnp.bfloat16)
    product = lax.dot_general(
        hidden, grads[0], (((0,), (0,)), ((), ())), preferred_element_type=jnp.float32
    )
    enc_grad = lax.psum(product, ("items", "book")) / (tok * lax.axis_size(("items", "book")))
    group_grads = lax.all_gather(jnp.stack(grads), "book", axis=1, tiled=True)
    rows_dev = shard_rows // lax.axis_size("items")

    def level_term(level, count):
        hits = code_hits(group_codes[level], offset, count)
        return -lax.dot_general(
            hits, group_grads[level], (((0,), (0,)), ((), ())), preferred_element_type=jnp.float32
        )

    tables = []
    for level in range(levels):
        tables.append(
            own_rows(lambda start, count, level=level: level_term(level, count), rows_dev, "items")
        )
    code_grad = jnp.stack(tables)[:, None]
    return (code_grad, enc_grad, history[-1])


def solution(mesh):
    in_specs = (P(("items", "book"), None), P(), P(None, "book", None), P(None, ("items", "book")))
    out_specs = (P(None, "book", "items", None), P(), P(("items", "book"), None))
    return jax.shard_map(
        on_device, mesh=mesh, in_specs=in_specs, out_specs=out_specs, check_vma=False
    )
```

profile of v0, /device:TPU:0, one launch (start us, length us, event | category | flops | bytes accessed | tf_op | source)
XLA Modules:
  0.0 578.7 jit_solution(3671878949450267147)
XLA Ops:
  7.2 12.8 %all_gather.6 = s32[3,1024]{1,0:T(4,128)S(1)} all-gather(s32[3,256]{1,0:T(4,128)} %param.7), channel_id=1, replica_groups=mesh['items'=32,'book'=4] {'book'}, dimensions={1}, use_global_device_ids=true | all-gather | bytes 15360 | tf_op jit(solution)/shard_map/all_gather | solution.py:23
  20.1 5.8 fusion.21
  25.8 3.7 fusion.24
  29.6 3.7 fusion.27
  33.3 2.3 pad_maximum_fusion
  35.7 0.2 all-gather.2.cloned.1.call-start
  35.9 52.7 %reduce-scatter.5.cloned.1.call-done = bf16[256,2304]{1,0:T(8,128)(2,1)} async-done(((bf16[1024,2304]{1,0:T(8,128)(2,1)}), bf16[256,2304]{1,0:T(8,128)(2,1)}) %reduce-scatter.5.cloned.1.call-update) | async-done | bytes 1179664 | tf_op jit(solution)/shard_map/reduce_scatter | solution.py:30
  88.6 1.4 convert_element_type.8
  90.1 0.6 add_convert_fusion
  90.7 0.2 convert_bitcast_fusion.1
  90.8 0.7 copy-done.1
  91.5 1.1 pad_maximum_fusion.1
  92.7 1.9 convolution_bitcast_fusion
  94.7 50.5 %all-gather.2.cloned.1.call-done = bf16[3,1024,768]{2,1,0:T(8,128)(2,1)} async-done(((bf16[3,256,768]{2,1,0:T(8,128)(2,1)}), bf16[3,1024,768]{2,1,0:T(8,128)(2,1)}) %all-gather.2.cloned.1.call-update) | async-done | bytes 4718608 | tf_op jit(solution)/shard_map/all_gather | solution.py:50
  145.2 7.8 %fusion.12 = f32[2048,768]{1,0:T(8,128)} fusion(s32[1024]{0:T(1024)S(1)} %bitcast.54, bf16[3,1024,768]{2,1,0:T(8,128)(2,1)} %all-gather.2.cloned.1.call-done), kind=kOutput, calls=%fused_computation.16 | convolution fusion | flops 3224895488 | bytes 7868416 | tf_op jit(solution)/shard_map/dot_general | solution.py:55
  153.1 7.8 %fusion.13 = f32[2048,768]{1,0:T(8,128)} fusion(s32[1024]{0:T(1024)S(1)} %bitcast.52, bf16[3,1024,768]{2,1,0:T(8,128)(2,1)} %all-gather.2.cloned.1.call-done), kind=kOutput, calls=%fused_computation.17 | convolution fusion | flops 3224895488 | bytes 7868416 | tf_op jit(solution)/shard_map/dot_general | solution.py:55
  160.9 7.8 %fusion.14 = f32[2048,768]{1,0:T(8,128)} fusion(s32[1024]{0:T(1024)S(1)} %bitcast.50, bf16[3,1024,768]{2,1,0:T(8,128)(2,1)} %all-gather.2.cloned.1.call-done), kind=kOutput, calls=%fused_computation.18 | convolution fusion | flops 3224895488 | bytes 7868416 | tf_op jit(solution)/shard_map/dot_general | solution.py:55
  168.7 133.7 %all-reduce.2.cloned.1.call-done = f32[768,768]{0,1:T(8,128)} async-done(((f32[768,768]{0,1:T(8,128)}), f32[768,768]{0,1:T(8,128)}) %all-reduce.2.cloned.1.call-update) | async-done | bytes 2359312 | tf_op jit(solution)/shard_map/psum | solution.py:49
  302.4 1.8 broadcast_multiply_fusion
  304.2 2.0 copy.11
  306.1 84.8 %reduce-scatter.7.cloned.1.call-done = f32[64,768]{1,0:T(8,128)} async-done(((f32[2048,768]{1,0:T(8,128)}), f32[64,768]{1,0:T(8,128)}) %reduce-scatter.7.cloned.1.call-update) | async-done | bytes 196624 | tf_op jit(solution)/shard_map/reduce_scatter | solution.py:9
  390.9 89.3 %reduce-scatter.9.cloned.1.call-done = f32[64,768]{1,0:T(8,128)} async-done(((f32[2048,768]{1,0:T(8,128)}), f32[64,768]{1,0:T(8,128)}) %reduce-scatter.9.cloned.1.call-update) | async-done | bytes 196624 | tf_op jit(solution)/shard_map/reduce_scatter | solution.py:9
  480.2 89.7 %reduce-scatter.11.cloned.1.call-done = f32[64,768]{1,0:T(8,128)} async-done(((f32[2048,768]{1,0:T(8,128)}), f32[64,768]{1,0:T(8,128)}) %reduce-scatter.11.cloned.1.call-update) | async-done | bytes 196624 | tf_op jit(solution)/shard_map/reduce_scatter | solution.py:9
  569.9 2.0 maximum_bitcast_fusion
  (19 shorter events, 0.3 us)
Async XLA Ops:
  7.2 82.9 %copy-start = (bf16[768,768]{1,0:T(8,128)(2,1)S(1)}, bf16[768,768]{1,0:T(8,128)(2,1)}, u32[]{:S(2)}) copy-start(bf16[768,768]{1,0:T(8,128)(2,1)} %param.5) | copy-start | bytes 3538948
  7.2 81.4 %reduce-scatter.5.cloned.1.call-start = ((), (), s32[]{:S(2)}) async-start(), calls=%async_computation.4 | async-start | bytes 5898240 | tf_op jit(solution)/shard_map/reduce_scatter | solution.py:30
  20.0 5.8 copy-start.3
  35.6 54.4 %copy-start.2 = (bf16[256,768]{1,0:T(8,128)(2,1)S(1)}, bf16[256,768]{1,0:T(8,128)(2,1)}, u32[]{:S(2)}) copy-start(bf16[256,768]{1,0:T(8,128)(2,1)} %param.4) | copy-start | bytes 1179652
  35.7 109.5 %all-gather.2.cloned.1.call-start = ((), (), s32[]{:S(2)}) async-start(), calls=%async_computation.5 | async-start | bytes 5898240 | tf_op jit(solution)/shard_map/all_gather | solution.py:50
  90.6 0.9 copy-start.1
  92.7 209.7 %all-reduce.2.cloned.1.call-start = ((), (), s32[]{:S(2)}) async-start(), calls=%async_computation.9 | async-start | bytes 4718592 | tf_op jit(solution)/shard_map/psum | solution.py:49
  94.7 296.2 %reduce-scatter.7.cloned.1.call-start = ((), (), s32[]{:S(2)}) async-start(), calls=%async_computation.6 | async-start | bytes 6488064 | tf_op jit(solution)/shard_map/reduce_scatter | solution.py:9
  153.0 327.2 %reduce-scatter.9.cloned.1.call-start = ((), (), s32[]{:S(2)}) async-start(), calls=%async_computation.7 | async-start | bytes 6488064 | tf_op jit(solution)/shard_map/reduce_scatter | solution.py:9
  160.8 409.0 %reduce-scatter.11.cloned.1.call-start = ((), (), s32[]{:S(2)}) async-start(), calls=%async_computation.8 | async-start | bytes 6488064 | tf_op jit(solution)/shard_map/reduce_scatter | solution.py:9
Sparse Core Ops, SparseCore 0:
  35.8 52.7 reduce-scatter.4
  92.8 52.3 all-gather.1
  150.6 151.7 all-reduce.1
  306.4 84.4 reduce-scatter.6
  394.5 85.6 reduce-scatter.8
  484.2 85.6 reduce-scatter.10
where the time goes:
time: 579 us
  waiting for transfers between devices  501 us (87%)
  matrix products  39 us (7%)
  between operations  14.2 us (2%)
  blocking collectives  12.8 us (2%)
  other arithmetic  8.85 us (2%)
    reduce_scatter x3, waiting for transfers between devices, own_rows(): lax.psum_scatter(portion(jnp.int32(0), count), axis, scatter_dimension=0,...  264 us
    psum x1, waiting for transfers between devices, on_device(): lax.psum(product, ('items', 'book'))  134 us
    reduce_scatter x1, waiting for transfers between devices, on_device(): lax.psum_scatter(jnp.concatenate(columns, axis=1).astype(jnp.bfloat16), '...  52.7 us
    all_gather x1, waiting for transfers between devices, on_device(): group_grads = lax.all_gather(jnp.stack(grads), 'book', axis=1, tiled=True)  50.5 us
    dot_general x3, matrix products, level_term(): lax.dot_general(hits, group_grads[level], (((0,), (0,)), ((), ())), prefe...  23.3 us
    dot_general x3, matrix products, on_device(): jnp.dot(hits, codebook[fetch_level], preferred_element_type=jnp.float32)  13.2 us
    all_gather x1, blocking collectives, on_device(): group_codes = lax.all_gather(codes, 'book', axis=1, tiled=True)  12.8 us
  transfers between devices with their start and end apart: 6, of which 6 were waited for; matrix products, arithmetic and copies ran while one was open for 5% of the time, Pallas kernels for 0%

commit v1 on v0

v1 whole, which is shorter than its diff:
```python
import jax
import jax.numpy as jnp
from jax import lax
from jax.experimental import pallas as pl
from jax.experimental.pallas import tpu as pltpu
from jax.sharding import PartitionSpec as P

MESH = pl.DeviceIdType.MESH
F32 = jnp.float32
BF16 = jnp.bfloat16
I32 = jnp.int32

TOK = 256
D = 768
LEVELS = 3
SHARD = 2048
CAP = 128
SLOTS = 4 * CAP
CW = 256
NCH = D // CW


def onehot(mask):
    return jnp.where(mask, 1.0, 0.0).astype(BF16)


def dot(a, b):
    return jnp.dot(a, b, preferred_element_type=F32)


def iota(shape, axis):
    return lax.broadcasted_iota(I32, shape, axis)


def kernel(
    hid, w, cb_hbm, codes, cg_out, enc_out, res_out,
    cb, code8, pk, rc, rcs, ut, u, oh, fs, rr, gs, gr, gsib, dd,
    s1s, s1r, s2s, s2r, e, ec, e1r, e2s, e2r, ey,
    cb_sem, pk_ss, pk_rs, rcs_ss, rcs_rs, f_ss, f_rs, g_ss, g_rs, sib_ss, sib_rs,
    s1_ss, s1_rs, s2_ss, s2_rs, ec_ss, ec_rs, e1_ss, e1_rs, e2_ss, e2_rs, ey_ss, ey_rs,
    a1_ss, a1_rs, a2_ss, a2_rs, a3_ss, a3_rs,
):
    i = lax.axis_index("items")
    y = lax.axis_index("book")
    c = i % 2
    x = (i // 2) % 4
    z = i // 8

    def at_y(k):
        return (i, (y + k) % 4)

    def at_x(k):
        return (z * 8 + ((x + k) % 4) * 2 + c, y)

    def at_z(k):
        return (((z + k) % 4) * 8 + x * 2 + c, y)

    sib = (z * 8 + x * 2 + (1 - c), y)

    def remote(src, dst, ss, rs, dev):
        return pltpu.make_async_remote_copy(
            src_ref=src, dst_ref=dst, send_sem=ss, recv_sem=rs, device_id=dev, device_id_type=MESH
        )

    cb_cp = [pltpu.make_async_copy(cb_hbm.at[l], cb.at[l], cb_sem.at[l]) for l in range(LEVELS)]
    for cp in cb_cp:
        cp.start()
    bar = pltpu.get_barrier_semaphore()
    for k in (1, 2, 3):
        pl.semaphore_signal(bar, inc=1, device_id=at_y(k), device_id_type=MESH)
        pl.semaphore_signal(bar, inc=1, device_id=at_x(k), device_id_type=MESH)
        pl.semaphore_signal(bar, inc=1, device_id=at_z(k), device_id_type=MESH)
    pl.semaphore_signal(bar, inc=1, device_id=sib, device_id_type=MESH)

    code8[...] = jnp.zeros_like(code8)
    code8[0:LEVELS, :] = codes[...]
    cv = code8[...]
    dist = ((cv >> 11) - y) & 3
    val = (cv & (SHARD - 1)) + 1
    tri = onehot(iota((TOK, TOK), 0) < iota((TOK, TOK), 1))
    pos = jnp.zeros((8, TOK), F32)
    for k in range(4):
        m = jnp.where(dist == k, 1.0, 0.0)
        pos = pos + m * (k * CAP + dot(m.astype(BF16), tri))
    pos_i = pos.astype(I32)
    pos_t = pos.T.astype(I32)
    hl = jnp.concatenate([(val >> 6).astype(F32), (val & 63).astype(F32)], axis=0).astype(BF16)
    pk[...] = jnp.zeros_like(pk)
    for l in range(LEVELS):
        ut[l] = onehot(iota((SLOTS, TOK), 0) == pos_i[l : l + 1, :])
        ul = onehot(iota((TOK, SLOTS), 1) == pos_t[:, l : l + 1])
        u[l] = ul
        pc = dot(hl, ul)
        row = pc[l : l + 1, :] * 64.0 + pc[8 + l : 9 + l, :]
        for k in range(4):
            pk[k, l : l + 1, :] = row[:, k * CAP : (k + 1) * CAP]
    rc[0] = pk[0]

    pl.semaphore_wait(bar, 10)
    pk_cp = [
        remote(pk.at[k], rc.at[4 - k], pk_ss.at[k - 1], pk_rs.at[k - 1], at_y(k)) for k in (1, 2, 3)
    ]
    for cp in pk_cp:
        cp.start()
    for cp in pk_cp:
        cp.wait()
    rcs_cp = remote(rc, rcs, rcs_ss, rcs_rs, sib)
    rcs_cp.start()

    held = jnp.concatenate([rc[k] for k in range(4)], axis=1)
    held_t = held.T.astype(I32)

    for l in range(LEVELS):
        col = held_t[:, l : l + 1]
        for h in range(2):
            oh[l, h * SLOTS : (h + 1) * SLOTS, :] = onehot(
                iota((SLOTS, 1024), 1) + (1 + h * 1024) == col
            )
    for cp in cb_cp:
        cp.wait()

    f_cp = []
    for ch in range(NCH):
        cols = slice(ch * CW, (ch + 1) * CW)

        def fetch(l, _, ch=ch, cols=cols):
            got = dot(oh[l, 0:SLOTS, :], cb[l, 0:1024, cols])
            got = got + dot(oh[l, SLOTS:, :], cb[l, 1024:2048, cols])
            got = got.astype(BF16)
            rr[ch, 0, l] = got[0:CAP]
            for k in (1, 2, 3):
                fs[ch, k - 1, l] = got[k * CAP : (k + 1) * CAP]
            return 0

        lax.fori_loop(0, LEVELS, fetch, 0)
        f_cp.append([
            remote(fs.at[ch, k - 1], rr.at[ch, 4 - k], f_ss.at[ch, k - 1], f_rs.at[ch, k - 1], at_y(k))
            for k in (2, 1, 3)
        ])
        if ch < 2:
            for cp in f_cp[ch]:
                cp.start()

    g_cp = []

    def chain(ch):
        cols = slice(ch * CW, (ch + 1) * CW)
        lifted = dot(hid[...], w[:, cols])
        res = []
        r = lifted
        for l in range(LEVELS):
            r = r - dot(u[l], rr[ch, :, l].reshape(SLOTS, CW))
            res.append(r)
        res_out[:, cols] = r
        carried = jnp.zeros_like(r)
        for l in reversed(range(LEVELS)):
            carried = carried + res[l]
            cl = carried.astype(BF16)
            packed = dot(ut[l], cl).astype(BF16)
            gr[ch, 0, l] = packed[0:CAP]
            for k in (1, 2, 3):
                gs[ch, k - 1, l] = packed[k * CAP : (k + 1) * CAP]
            if l == 0:
                prod = lax.dot_general(
                    hid[...], cl, (((0,), (0,)), ((), ())), preferred_element_type=F32
                )
                e[:, :, :, :, cols] = prod.reshape(2, 4, 4, 24, CW)
        cps = [
            remote(gs.at[ch, k - 1], gr.at[ch, 4 - k], g_ss.at[ch, k - 1], g_rs.at[ch, k - 1], at_y(k))
            for k in (2, 1, 3)
        ]
        for cp in cps:
            cp.start()
        g_cp.append(cps)

    for cp in f_cp[0]:
        cp.wait()
    chain(0)
    for cp in f_cp[1]:
        cp.wait()
    for cp in f_cp[2]:
        cp.start()
    chain(1)

    rcs_cp.wait()
    for l in range(LEVELS):
        for h, src in enumerate((rc, rcs)):
            slot_code = jnp.concatenate(
                [src[k, l : l + 1, :] for k in range(4)], axis=1
            ).astype(I32)
            rows = iota((1024, SLOTS), 0)
            code = ((rows >> 6) << 7) + c * 64 + (rows & 63) + 1
            oh[l, :, h * SLOTS : (h + 1) * SLOTS] = onehot(code == slot_code)

    for cp in g_cp[0]:
        cp.wait()
    sib_cp = []

    def to_sib(ch):
        cp = remote(gr.at[ch], gsib.at[ch], sib_ss.at[ch], sib_rs.at[ch], sib)
        cp.start()
        sib_cp.append(cp)

    to_sib(0)

    for cp in f_cp[2]:
        cp.wait()
    chain(2)
    ec_cp = remote(e.at[1 - c], ec, ec_ss, ec_rs, sib)
    ec_cp.start()

    s1_cp = []

    def stage1(ch):
        sib_cp[ch].wait()

        def dense(l, _):
            acc = dot(oh[l, :, 0:SLOTS], gr[ch, :, l].reshape(SLOTS, CW))
            acc = acc + dot(oh[l, :, SLOTS:], gsib[ch, :, l].reshape(SLOTS, CW))
            dd[ch % 2, l] = acc.reshape(4, 4, 64, CW)
            for k in (1, 2, 3):
                s1s[ch, 0, k - 1, l] = dd[ch % 2, l, :, (x + k) % 4, 0:32, :].astype(BF16)
                s1s[ch, 1, k - 1, l] = dd[ch % 2, l, (z + k) % 4, :, 32:64, :].astype(BF16)
            return 0

        lax.fori_loop(0, LEVELS, dense, 0)
        cps = []
        for k in (2, 1, 3):
            for h, at in enumerate((at_x, at_z)):
                cps.append(remote(
                    s1s.at[ch, h, k - 1], s1r.at[ch, h, k - 1],
                    s1_ss.at[ch, h, k - 1], s1_rs.at[ch, h, k - 1], at(k),
                ))
        for cp in cps:
            cp.start()
        s1_cp.append(cps)

    s2_cp = []

    def stage2(ch):
        for cp in s1_cp[ch]:
            cp.wait()

        def sums(l, _):
            tx = dd[ch % 2, l, :, x, 0:32, :]
            tz = dd[ch % 2, l, z, :, 32:64, :]
            for k in range(3):
                tx = tx + s1r[ch, 0, k, l].astype(F32)
                tz = tz + s1r[ch, 1, k, l].astype(F32)
            s2s[ch, 0, :, l] = tx
            s2s[ch, 1, :, l] = tz
            return 0

        lax.fori_loop(0, LEVELS, sums, 0)
        cps = []
        for k in (2, 1, 3):
            cps.append(remote(
                s2s.at[ch, 0, (z + k) % 4], s2r.at[ch, 0, k - 1],
                s2_ss.at[ch, 0, k - 1], s2_rs.at[ch, 0, k - 1], at_z(k),
            ))
            cps.append(remote(
                s2s.at[ch, 1, (x + k) % 4], s2r.at[ch, 1, k - 1],
                s2_ss.at[ch, 1, k - 1], s2_rs.at[ch, 1, k - 1], at_x(k),
            ))
        for cp in cps:
            cp.start()
        s2_cp.append(cps)

    def finish(ch):
        cols = slice(ch * CW, (ch + 1) * CW)
        for cp in s2_cp[ch]:
            cp.wait()
        t0 = s2s[ch, 0, z]
        t1 = s2s[ch, 1, x]
        for k in range(3):
            t0 = t0 + s2r[ch, 0, k]
            t1 = t1 + s2r[ch, 1, k]
        cg_out[:, 0:32, cols] = -t0
        cg_out[:, 32:64, cols] = -t1

    stage1(0)

    ec_cp.wait()
    e[c] = e[c] + ec[...]
    H = D // 2
    e1_cp = []
    for k in (2, 1, 3):
        e1_cp.append(remote(
            e.at[c, :, (x + k) % 4, :, 0:H], e1r.at[0, k - 1],
            e1_ss.at[0, k - 1], e1_rs.at[0, k - 1], at_x(k),
        ))
        e1_cp.append(remote(
            e.at[c, (z + k) % 4, :, :, H:D], e1r.at[1, k - 1],
            e1_ss.at[1, k - 1], e1_rs.at[1, k - 1], at_z(k),
        ))
    for cp in e1_cp:
        cp.start()

    for cp in g_cp[1]:
        cp.wait()
    to_sib(1)
    stage2(0)
    stage1(1)

    for cp in e1_cp:
        cp.wait()
    t0 = e[c, :, x, :, 0:H]
    t1 = e[c, z, :, :, H:D]
    for k in range(3):
        t0 = t0 + e1r[0, k]
        t1 = t1 + e1r[1, k]
    e2s[0] = t0
    e2s[1] = t1
    e2_cp = []
    for k in (2, 1, 3):
        e2_cp.append(remote(
            e2s.at[0, (z + k) % 4], e2r.at[0, k - 1], e2_ss.at[0, k - 1], e2_rs.at[0, k - 1], at_z(k)
        ))
        e2_cp.append(remote(
            e2s.at[1, (x + k) % 4], e2r.at[1, k - 1], e2_ss.at[1, k - 1], e2_rs.at[1, k - 1], at_x(k)
        ))
    for cp in e2_cp:
        cp.start()
    for cp in g_cp[2]:
        cp.wait()
    to_sib(2)
    finish(0)
    for cp in e2_cp:
        cp.wait()
    t0 = e2s[0, z]
    t1 = e2s[1, x]
    for k in range(3):
        t0 = t0 + e2r[0, k]
        t1 = t1 + e2r[1, k]
    ey[y, :, 0:H] = t0
    ey[y, :, H:D] = t1
    ey_cp = [
        remote(ey.at[y], ey.at[y], ey_ss.at[k - 1], ey_rs.at[k - 1], at_y(k)) for k in (2, 1, 3)
    ]
    for cp in ey_cp:
        cp.start()
    stage2(1)
    stage1(2)
    for cp in ey_cp:
        cp.wait()
    enc_out[c, z, x] = (((ey[0] + ey[1]) + ey[2]) + ey[3]) * (1.0 / (TOK * 128))

    def gather(step, ss, rs):
        cps = []
        for k in (2, 1, 3):
            if step == 1:
                va = enc_out.at[c, z, x, :, 0:H]
                vb = enc_out.at[c, z, x, :, H:D]
                da, db = at_x(k), at_z(k)
            else:
                va = enc_out.at[c, z, :, :, 0:H]
                vb = enc_out.at[c, :, x, :, H:D]
                da, db = at_z(k), at_x(k)
            cps.append(remote(va, va, ss.at[0, k - 1], rs.at[0, k - 1], da))
            cps.append(remote(vb, vb, ss.at[1, k - 1], rs.at[1, k - 1], db))
        for cp in cps:
            cp.start()
        return cps

    a1_cp = gather(1, a1_ss, a1_rs)
    finish(1)
    for cp in a1_cp:
        cp.wait()
    a2_cp = gather(2, a2_ss, a2_rs)
    stage2(2)
    for cp in a2_cp:
        cp.wait()
    a3_cp = remote(enc_out.at[c], enc_out.at[c], a3_ss, a3_rs, sib)
    a3_cp.start()
    finish(2)
    a3_cp.wait()


def on_device(hidden, enc_weight, codebook, codes):
    dma = pltpu.SemaphoreType.DMA
    vmem = pltpu.VMEM
    H = D // 2
    scratch = [
        vmem((LEVELS, SHARD, D), BF16),
        vmem((8, TOK), I32),
        vmem((4, 8, CAP), F32),
        vmem((4, 8, CAP), F32),
        vmem((4, 8, CAP), F32),
        vmem((LEVELS, SLOTS, TOK), BF16),
        vmem((LEVELS, TOK, SLOTS), BF16),
        vmem((LEVELS, 1024, 1024), BF16),
        vmem((NCH, 3, LEVELS, CAP, CW), BF16),
        vmem((NCH, 4, LEVELS, CAP, CW), BF16),
        vmem((NCH, 3, LEVELS, CAP, CW), BF16),
        vmem((NCH, 4, LEVELS, CAP, CW), BF16),
        vmem((NCH, 4, LEVELS, CAP, CW), BF16),
        vmem((2, LEVELS, 4, 4, 64, CW), F32),
        vmem((NCH, 2, 3, LEVELS, 4, 32, CW), BF16),
        vmem((NCH, 2, 3, LEVELS, 4, 32, CW), BF16),
        vmem((NCH, 2, 4, LEVELS, 32, CW), F32),
        vmem((NCH, 2, 3, LEVELS, 32, CW), F32),
        vmem((2, 4, 4, 24, D), F32),
        vmem((4, 4, 24, D), F32),
        vmem((2, 3, 4, 24, H), F32),
        vmem((2, 4, 24, H), F32),
        vmem((2, 3, 24, H), F32),
        vmem((4, 24, D), F32),
        dma((LEVELS,)),
        dma((3,)), dma((3,)), dma, dma,
        dma((NCH, 3)), dma((NCH, 3)), dma((NCH, 3)), dma((NCH, 3)),
        dma((NCH,)), dma((NCH,)),
        dma((NCH, 2, 3)), dma((NCH, 2, 3)), dma((NCH, 2, 3)), dma((NCH, 2, 3)),
        dma, dma,
        dma((2, 3)), dma((2, 3)), dma((2, 3)), dma((2, 3)),
        dma((3,)), dma((3,)),
        dma((2, 3)), dma((2, 3)), dma((2, 3)), dma((2, 3)),
        dma, dma,
    ]
    in_vmem = pl.BlockSpec(memory_space=pltpu.VMEM)
    code_grad, enc_grad, last = pl.pallas_call(
        kernel,
        out_shape=(
            jax.ShapeDtypeStruct((LEVELS, 64, D), F32),
            jax.ShapeDtypeStruct((2, 4, 4, 24, D), F32),
            jax.ShapeDtypeStruct((TOK, D), F32),
        ),
        in_specs=[in_vmem, in_vmem, pl.BlockSpec(memory_space=pl.ANY), in_vmem],
        out_specs=(in_vmem, in_vmem, in_vmem),
        scratch_shapes=scratch,
        compiler_params=pltpu.CompilerParams(
            collective_id=0, has_side_effects=True, vmem_limit_bytes=62 * 2**20
        ),
        cost_estimate=pl.CostEstimate(flops=13 * 10**9, bytes_accessed=16 * 10**6, transcendentals=0),
        name="quantizer_step",
    )(hidden, enc_weight, codebook, codes)
    return code_grad[:, None], enc_grad.reshape(D, D), last


def solution(mesh):
    in_specs = (P(("items", "book"), None), P(), P(None, "book", None), P(None, ("items", "book")))
    out_specs = (P(None, "book", "items", None), P(), P(("items", "book"), None))
    return jax.shard_map(
        on_device, mesh=mesh, in_specs=in_specs, out_specs=out_specs, check_vma=False
    )
```

time: 579 us -> 126 us (0.22)
  waiting for transfers between devices: 501 us -> 0 us
  Pallas kernels: 0 us -> 118 us
  matrix products: 39 us -> 0 us
  between operations: 14.2 us -> 0.64 us
  blocking collectives: 12.8 us -> 0 us
  other arithmetic: 8.85 us -> 0 us
    reduce_scatter x4 -> x0, waiting for transfers between devices: 316 us -> none  [the longest x3 264 us: own_rows(): lax.psum_scatter(portion(jnp.int32(0), count), axis, scatter_dimension=0,...]
    psum x1 -> x0, waiting for transfers between devices: 134 us -> none  [on_device(): lax.psum(product, ('items', 'book'))]
    pallas_call x0 -> x1, Pallas kernels: none -> 118 us  [on_device(): pl.pallas_call(kernel, out_shape=(jax.ShapeDtypeStruct((LEVELS, 64, D), F...]
    all_gather x1 -> x0, waiting for transfers between devices: 50.5 us -> none  [on_device(): group_grads = lax.all_gather(jnp.stack(grads), 'book', axis=1, tiled=True)]
    dot_general x8 -> x0, matrix products: 39 us -> none  [the longest x3 23.3 us: level_term(): lax.dot_general(hits, group_grads[level], (((0,), (0,)), ((), ())), prefe...]
    all_gather x1 -> x0, blocking collectives: 12.8 us -> none  [on_device(): group_codes = lax.all_gather(codes, 'book', axis=1, tiled=True)]
  transfers between devices with their start and end apart: 6 -> 0, of which waited for: 6 -> 0; matrix products, arithmetic and copies ran while one was open for 5% -> 0% of each run, Pallas kernels for 0% -> 0%
where the time goes in v1:
time: 126 us; the launch traced here: 125 us
  Pallas kernels  118 us (94%)
  local copies, waits for them, and re-layouts  6.1 us (5%)
    pallas_call x1, Pallas kernels, on_device(): pl.pallas_call(kernel, out_shape=(jax.ShapeDtypeStruct((LEVELS, 64, D), F...  118 us
    unnamed x5, local copies, waits for them, and re-layouts  6.1 us

profile of v1, /device:TPU:0, one launch (start us, length us, event | category | flops | bytes accessed | tf_op | source)
XLA Modules:
  0.0 124.6 jit_solution(13480968394408063759)
XLA Ops:
  0.6 117.8 %quantizer_step.1 = (f32[3,64,768]{2,1,0:T(8,128)}, f32[2,4,4,24,768]{4,3,2,1,0:T(8,128)}, f32[256,768]{1,0:T(8,128)}) custom-call(bf16[256,768]{1,0:T(8,128)(2,1)} %hid.1, bf16[768,768]{1,0:T(8,128)(2,1)} %w.1, bf16[3,2048,768]{2,1,0:T(8,128)(2,1)} %cb_hbm.1, s32[3,256]{1,0:T(4,128)} %codes.1), custom_call_target="tpu_custom_call" | custom-call | flops 12999999488 | bytes 16000000 | tf_op jit(solution)/shard_map/quantizer_step/pallas_call | solution.py:420
  118.5 1.9 %copy.11 = f32[3,1,64,768]{3,2,1,0:T(8,128)} copy(f32[3,1,64,768]{3,2,1,0:T(8,128)} %bitcast.5) | data formatting | bytes 1179648
  120.4 0.0 copy-start
  120.4 3.3 %copy.12 = f32[768,768]{1,0:T(8,128)} copy(f32[768,768]{1,0:T(8,128)} %bitcast.4) | data formatting | bytes 4718592
  123.7 0.0 copy-done
  123.7 0.9 copy.13
Async XLA Ops:
  120.4 3.3 %copy-start = (f32[256,768]{1,0:T(8,128)S(1)}, f32[256,768]{1,0:T(8,128)}, u32[]{:S(2)}) copy-start(f32[256,768]{1,0:T(8,128)} %get-tuple-element.17) | copy-start | bytes 2359300

commit v2 on v0

v2 whole, which is shorter than its diff:
```python
import jax
import jax.numpy as jnp
from jax import lax
from jax.experimental import pallas as pl
from jax.experimental.pallas import tpu as pltpu
from jax.sharding import PartitionSpec as P

MESH = pl.DeviceIdType.MESH
F32 = jnp.float32
BF16 = jnp.bfloat16
I32 = jnp.int32

TOK = 256
D = 768
LEVELS = 3
SHARD = 2048
CAP = 128
SLOTS = 4 * CAP
CW = 256
NCH = D // CW
UNITS = [(ch, l) for ch in range(NCH) for l in (2, 1, 0)]
RING = 6


def onehot(mask):
    return jnp.where(mask, 1.0, 0.0).astype(BF16)


def dot(a, b):
    return jnp.dot(a, b, preferred_element_type=F32)


def iota(shape, axis):
    return lax.broadcasted_iota(I32, shape, axis)


def kernel(
    hid_hbm, w_hbm, cb_hbm, codes, cg_hbm, enc_hbm, res_hbm,
    hid, w, cb, code8, pk, rc, rcs, ut, u, oh, fs, rr, gs, gr, gsib, dd,
    fars, farr, nears, nearr, s2s, s2r, e, ec, e1r, e2s, e2r, ey, cg_out, enc_out, res_out,
    in_sem, cb_sem, out_sem, pk_ss, pk_rs, rcs_ss, rcs_rs, f_ss, f_rs, g_ss, g_rs, sib_ss, sib_rs,
    far_ss, far_rs, near_ss, near_rs, s2_ss, s2_rs, ec_ss, ec_rs, e1_ss, e1_rs, e2_ss, e2_rs,
    ey_ss, ey_rs, a1_ss, a1_rs, a2_ss, a2_rs, a3_ss, a3_rs,
):
    i = lax.axis_index("items")
    y = lax.axis_index("book")
    c = i % 2
    x = (i // 2) % 4
    z = i // 8

    def at_y(k):
        return (i, (y + k) % 4)

    def at_x(k):
        return (z * 8 + ((x + k) % 4) * 2 + c, y)

    def at_z(k):
        return (((z + k) % 4) * 8 + x * 2 + c, y)

    sib = (z * 8 + x * 2 + (1 - c), y)

    def remote(src, dst, ss, rs, dev):
        return pltpu.make_async_remote_copy(
            src_ref=src, dst_ref=dst, send_sem=ss, recv_sem=rs, device_id=dev, device_id_type=MESH
        )

    def start(cps):
        for cp in cps:
            cp.start()
        return cps

    def wait(cps):
        for cp in cps:
            cp.wait()

    bar = pltpu.get_barrier_semaphore()
    for k in (1, 2, 3):
        pl.semaphore_signal(bar, inc=1, device_id=at_y(k), device_id_type=MESH)
        pl.semaphore_signal(bar, inc=1, device_id=at_x(k), device_id_type=MESH)
        pl.semaphore_signal(bar, inc=1, device_id=at_z(k), device_id_type=MESH)
    pl.semaphore_signal(bar, inc=1, device_id=sib, device_id_type=MESH)
    cb_cp = start([
        pltpu.make_async_copy(cb_hbm.at[l], cb.at[l], cb_sem.at[l]) for l in range(LEVELS)
    ])
    in_cp = start([
        pltpu.make_async_copy(hid_hbm, hid, in_sem.at[0]),
        pltpu.make_async_copy(w_hbm, w, in_sem.at[1]),
    ])

    code8[...] = jnp.zeros_like(code8)
    code8[0:LEVELS, :] = codes[...]
    cv = code8[...]
    dist = ((cv >> 11) - y) & 3
    val = (cv & (SHARD - 1)) + 1
    tri = onehot(iota((TOK, TOK), 0) < iota((TOK, TOK), 1))
    pos = jnp.zeros((8, TOK), F32)
    for k in range(4):
        m = jnp.where(dist == k, 1.0, 0.0)
        pos = pos + m * (k * CAP + dot(m.astype(BF16), tri))
    pos_i = pos.astype(I32)
    pos_t = pos.T.astype(I32)
    hl = jnp.concatenate([(val >> 6).astype(F32), (val & 63).astype(F32)], axis=0).astype(BF16)
    pk[...] = jnp.zeros_like(pk)
    for l in range(LEVELS):
        ul = onehot(iota((TOK, SLOTS), 1) == pos_t[:, l : l + 1])
        u[l] = ul
        pc = dot(hl, ul)
        row = pc[l : l + 1, :] * 64.0 + pc[8 + l : 9 + l, :]
        for k in range(4):
            pk[k, l : l + 1, :] = row[:, k * CAP : (k + 1) * CAP]
    rc[0] = pk[0]

    pl.semaphore_wait(bar, 10)
    pk_cp = start([
        remote(pk.at[k], rc.at[4 - k], pk_ss.at[k - 1], pk_rs.at[k - 1], at_y(k)) for k in (2, 1, 3)
    ])
    for l in range(LEVELS):
        ut[l] = onehot(iota((SLOTS, TOK), 0) == pos_i[l : l + 1, :])
    wait(pk_cp)
    rcs_cp = remote(rc, rcs, rcs_ss, rcs_rs, sib)
    rcs_cp.start()

    held = jnp.concatenate([rc[k] for k in range(4)], axis=1)
    held_t = held.T.astype(I32)

    def fetch_copies(ch, l):
        return [
            remote(
                fs.at[ch, l, k - 1], rr.at[ch, l, 4 - k],
                f_ss.at[ch, l, k - 1], f_rs.at[ch, l, k - 1], at_y(k),
            )
            for k in (2, 1, 3)
        ]

    def fetch(ch, l):
        cols = slice(ch * CW, (ch + 1) * CW)
        got = dot(oh[l, 0:SLOTS, :], cb[l, 0:1024, cols])
        got = got + dot(oh[l, SLOTS:, :], cb[l, 1024:2048, cols])
        got = got.astype(BF16)
        rr[ch, l, 0] = got[0:CAP]
        for k in (1, 2, 3):
            fs[ch, l, k - 1] = got[k * CAP : (k + 1) * CAP]

    f_cp = [[], [], []]
    for l in range(LEVELS):
        col = held_t[:, l : l + 1]
        for h in range(2):
            oh[l, h * SLOTS : (h + 1) * SLOTS, :] = onehot(
                iota((SLOTS, 1024), 1) + (1 + h * 1024) == col
            )
        cb_cp[l].wait()
        fetch(0, l)
        f_cp[0] += start(fetch_copies(0, l))
    for ch in (1, 2):
        for l in range(LEVELS):
            fetch(ch, l)
            f_cp[ch] += fetch_copies(ch, l)
            if ch == 1:
                start(f_cp[1][-3:])
    wait(in_cp)

    g_cp = {}
    ec_cp = {}

    def chain(ch):
        cols = slice(ch * CW, (ch + 1) * CW)
        wait(f_cp[ch])
        r = dot(hid[...], w[:, cols])
        res = []
        for l in range(LEVELS):
            r = r - dot(u[l], rr[ch, l].reshape(SLOTS, CW))
            res.append(r)
        carried = jnp.zeros_like(r)
        for l in reversed(range(LEVELS)):
            carried = carried + res[l]
            cl = carried.astype(BF16)
            packed = dot(ut[l], cl).astype(BF16)
            gr[ch, l, 0] = packed[0:CAP]
            for k in (1, 2, 3):
                gs[ch, l, k - 1] = packed[k * CAP : (k + 1) * CAP]
            g_cp[ch, l] = start([
                remote(
                    gs.at[ch, l, k - 1], gr.at[ch, l, 4 - k],
                    g_ss.at[ch, l, k - 1], g_rs.at[ch, l, k - 1], at_y(k),
                )
                for k in (2, 1, 3)
            ])
        res_out[:, cols] = r
        prod = lax.dot_general(
            hid[...], cl, (((0,), (0,)), ((), ())), preferred_element_type=F32
        )
        e[ch] = prod.reshape(2, 4, 4, 24, CW)
        ec_cp[ch] = start([
            remote(e.at[ch, 1 - c], ec.at[ch], ec_ss.at[ch], ec_rs.at[ch], sib)
        ])

    e1_cp = {}
    e2_cp = {}
    HW = CW // 2

    def enc_b(ch):
        wait(ec_cp[ch])
        e[ch, c] = e[ch, c] + ec[ch]
        cps = []
        for k in (2, 1, 3):
            cps.append(remote(
                e.at[ch, c, :, (x + k) % 4, :, 0:HW], e1r.at[ch, 0, k - 1],
                e1_ss.at[ch, 0, k - 1], e1_rs.at[ch, 0, k - 1], at_x(k),
            ))
            cps.append(remote(
                e.at[ch, c, (z + k) % 4, :, :, HW:CW], e1r.at[ch, 1, k - 1],
                e1_ss.at[ch, 1, k - 1], e1_rs.at[ch, 1, k - 1], at_z(k),
            ))
        e1_cp[ch] = start(cps)

    def enc_c(ch):
        wait(e1_cp[ch])
        t0 = e[ch, c, :, x, :, 0:HW]
        t1 = e[ch, c, z, :, :, HW:CW]
        for k in range(3):
            t0 = t0 + e1r[ch, 0, k]
            t1 = t1 + e1r[ch, 1, k]
        e2s[ch, 0] = t0
        e2s[ch, 1] = t1
        cps = []
        for k in (2, 1, 3):
            cps.append(remote(
                e2s.at[ch, 0, (z + k) % 4], e2r.at[ch, 0, k - 1],
                e2_ss.at[ch, 0, k - 1], e2_rs.at[ch, 0, k - 1], at_z(k),
            ))
            cps.append(remote(
                e2s.at[ch, 1, (x + k) % 4], e2r.at[ch, 1, k - 1],
                e2_ss.at[ch, 1, k - 1], e2_rs.at[ch, 1, k - 1], at_x(k),
            ))
        e2_cp[ch] = start(cps)

    def enc_d(ch):
        wait(e2_cp[ch])
        t0 = e2s[ch, 0, z]
        t1 = e2s[ch, 1, x]
        for k in range(3):
            t0 = t0 + e2r[ch, 0, k]
            t1 = t1 + e2r[ch, 1, k]
        ey[y, :, ch * CW : ch * CW + HW] = t0
        ey[y, :, ch * CW + HW : (ch + 1) * CW] = t1

    sib_cp, far_cp, near_cp, s2_cp, out_cp = {}, {}, {}, {}, []

    def unit_a(n):
        ch, l = UNITS[n]
        wait(g_cp[ch, l])
        sib_cp[n] = start([
            remote(gr.at[ch, l], gsib.at[ch, l], sib_ss.at[ch, l], sib_rs.at[ch, l], sib)
        ])

    def unit_b(n):
        ch, l = UNITS[n]
        q = n % RING
        acc = dot(oh[l, :, 0:SLOTS], gr[ch, l].reshape(SLOTS, CW))
        wait(sib_cp[n])
        acc = acc + dot(oh[l, :, SLOTS:], gsib[ch, l].reshape(SLOTS, CW))
        dd[q] = acc.reshape(4, 4, 64, CW)
        x2 = (x + 2) % 4
        z2 = (z + 2) % 4
        cps = []
        for d, k in enumerate((1, 3)):
            fars[n, 0, d] = dd[q, 2 * d : 2 * d + 2, x2, 0:32, :].astype(BF16)
            fars[n, 1, d] = dd[q, z2, 2 * d : 2 * d + 2, 32:64, :].astype(BF16)
            for h, at in enumerate((at_x, at_z)):
                cps.append(remote(
                    fars.at[n, h, d], farr.at[n, h, d],
                    far_ss.at[n, h, d], far_rs.at[n, h, d], at(k),
                ))
        far_cp[n] = start(cps)

    def unit_c(n):
        q = n % RING
        wait(far_cp[n])
        cps = []
        for d, k in enumerate((1, 3)):
            xk = (x + k) % 4
            zk = (z + k) % 4
            a, b = 2 * d, 2 - 2 * d
            nears[n, 0, d, a : a + 2] = (
                dd[q, a : a + 2, xk, 0:32, :] + farr[n, 0, d].astype(F32)
            ).astype(BF16)
            nears[n, 0, d, b : b + 2] = dd[q, b : b + 2, xk, 0:32, :].astype(BF16)
            nears[n, 1, d, a : a + 2] = (
                dd[q, zk, a : a + 2, 32:64, :] + farr[n, 1, d].astype(F32)
            ).astype(BF16)
            nears[n, 1, d, b : b + 2] = dd[q, zk, b : b + 2, 32:64, :].astype(BF16)
            for h, at in enumerate((at_x, at_z)):
                cps.append(remote(
                    nears.at[n, h, d], nearr.at[n, h, d],
                    near_ss.at[n, h, d], near_rs.at[n, h, d], at(k),
                ))
        near_cp[n] = start(cps)

    def unit_d(n):
        q = n % RING
        wait(near_cp[n])
        tx = dd[q, :, x, 0:32, :]
        tz = dd[q, z, :, 32:64, :]
        for d in range(2):
            tx = tx + nearr[n, 0, d].astype(F32)
            tz = tz + nearr[n, 1, d].astype(F32)
        s2s[n, 0] = tx
        s2s[n, 1] = tz
        cps = []
        for k in (2, 1, 3):
            cps.append(remote(
                s2s.at[n, 0, (z + k) % 4], s2r.at[n, 0, k - 1],
                s2_ss.at[n, 0, k - 1], s2_rs.at[n, 0, k - 1], at_z(k),
            ))
            cps.append(remote(
                s2s.at[n, 1, (x + k) % 4], s2r.at[n, 1, k - 1],
                s2_ss.at[n, 1, k - 1], s2_rs.at[n, 1, k - 1], at_x(k),
            ))
        s2_cp[n] = start(cps)

    def unit_e(n):
        ch, l = UNITS[n]
        cols = slice(ch * CW, (ch + 1) * CW)
        wait(s2_cp[n])
        t0 = s2s[n, 0, z]
        t1 = s2s[n, 1, x]
        for k in range(3):
            t0 = t0 + s2r[n, 0, k]
            t1 = t1 + s2r[n, 1, k]
        cg_out[l, 0:32, cols] = -t0
        cg_out[l, 32:64, cols] = -t1

    def step(t):
        for lag, op in enumerate((unit_a, unit_b, unit_c, unit_d, unit_e)):
            if 0 <= t - lag < len(UNITS):
                op(t - lag)

    H = D // 2

    def gather(turn, ss, rs):
        cps = []
        for k in (2, 1, 3):
            if turn == 1:
                va = enc_out.at[c, z, x, :, 0:H]
                vb = enc_out.at[c, z, x, :, H:D]
                da, db = at_x(k), at_z(k)
            else:
                va = enc_out.at[c, z, :, :, 0:H]
                vb = enc_out.at[c, :, x, :, H:D]
                da, db = at_z(k), at_x(k)
            cps.append(remote(va, va, ss.at[0, k - 1], rs.at[0, k - 1], da))
            cps.append(remote(vb, vb, ss.at[1, k - 1], rs.at[1, k - 1], db))
        return start(cps)

    chain(0)
    rcs_cp.wait()
    for l in range(LEVELS):
        for h, src in enumerate((rc, rcs)):
            slot_code = jnp.concatenate(
                [src[k, l : l + 1, :] for k in range(4)], axis=1
            ).astype(I32)
            rows = iota((1024, SLOTS), 0)
            code = ((rows >> 6) << 7) + c * 64 + (rows & 63) + 1
            oh[l, :, h * SLOTS : (h + 1) * SLOTS] = onehot(code == slot_code)
    enc_b(0)
    wait(f_cp[1])
    start(f_cp[2])
    f_cp[1] = []
    chain(1)
    enc_c(0)
    enc_b(1)
    step(0)
    enc_d(0)
    enc_c(1)
    step(1)
    enc_d(1)
    step(2)
    chain(2)
    out_cp += start([pltpu.make_async_copy(res_out, res_hbm, out_sem.at[0])])
    step(3)
    enc_b(2)
    step(4)
    enc_c(2)
    step(5)
    enc_d(2)
    ey_cp = start([
        remote(ey.at[y], ey.at[y], ey_ss.at[k - 1], ey_rs.at[k - 1], at_y(k)) for k in (2, 1, 3)
    ])
    step(6)
    wait(ey_cp)
    enc_out[c, z, x] = (((ey[0] + ey[1]) + ey[2]) + ey[3]) * (1.0 / (TOK * 128))
    a1_cp = gather(1, a1_ss, a1_rs)
    step(7)
    wait(a1_cp)
    a2_cp = gather(2, a2_ss, a2_rs)
    step(8)
    step(9)
    wait(a2_cp)
    a3_cp = start([remote(enc_out.at[c], enc_out.at[c], a3_ss, a3_rs, sib)])
    step(10)
    wait(a3_cp)
    out_cp += start([pltpu.make_async_copy(enc_out, enc_hbm, out_sem.at[1])])
    step(11)
    step(12)
    out_cp += start([pltpu.make_async_copy(cg_out, cg_hbm, out_sem.at[2])])
    wait(out_cp)


def store(a_hbm, b_hbm, c_hbm, ao, bo, co, av, bv, cv, in_sem, out_sem):
    pieces = []
    for k in range(2):
        for q in range(2):
            part = (k, pl.ds(2 * q, 2))
            pieces.append((b_hbm.at[part], bv.at[part], bo.at[part]))
    pieces += [(a_hbm, av, ao), (c_hbm, cv, co)]
    loads = [pltpu.make_async_copy(s, v, in_sem.at[n]) for n, (s, v, o) in enumerate(pieces)]
    stores = [pltpu.make_async_copy(v, o, out_sem.at[n]) for n, (s, v, o) in enumerate(pieces)]
    for cp in loads:
        cp.start()
    for load, back in zip(loads, stores):
        load.wait()
        back.start()
    for cp in stores:
        cp.wait()


def on_device(hidden, enc_weight, codebook, codes):
    dma = pltpu.SemaphoreType.DMA
    vmem = pltpu.VMEM
    n = len(UNITS)
    scratch = [
        vmem((TOK, D), BF16),
        vmem((D, D), BF16),
        vmem((LEVELS, SHARD, D), BF16),
        vmem((8, TOK), I32),
        vmem((4, 8, CAP), F32),
        vmem((4, 8, CAP), F32),
        vmem((4, 8, CAP), F32),
        vmem((LEVELS, SLOTS, TOK), BF16),
        vmem((LEVELS, TOK, SLOTS), BF16),
        vmem((LEVELS, 1024, 1024), BF16),
        vmem((NCH, LEVELS, 3, CAP, CW), BF16),
        vmem((NCH, LEVELS, 4, CAP, CW), BF16),
        vmem((NCH, LEVELS, 3, CAP, CW), BF16),
        vmem((NCH, LEVELS, 4, CAP, CW), BF16),
        vmem((NCH, LEVELS, 4, CAP, CW), BF16),
        vmem((RING, 4, 4, 64, CW), F32),
        vmem((n, 2, 2, 2, 32, CW), BF16),
        vmem((n, 2, 2, 2, 32, CW), BF16),
        vmem((n, 2, 2, 4, 32, CW), BF16),
        vmem((n, 2, 2, 4, 32, CW), BF16),
        vmem((n, 2, 4, 32, CW), F32),
        vmem((n, 2, 3, 32, CW), F32),
        vmem((NCH, 2, 4, 4, 24, CW), F32),
        vmem((NCH, 4, 4, 24, CW), F32),
        vmem((NCH, 2, 3, 4, 24, CW // 2), F32),
        vmem((NCH, 2, 4, 24, CW // 2), F32),
        vmem((NCH, 2, 3, 24, CW // 2), F32),
        vmem((4, 24, D), F32),
        vmem((LEVELS, 64, D), F32),
        vmem((2, 4, 4, 24, D), F32),
        vmem((TOK, D), F32),
        dma((2,)), dma((LEVELS,)), dma((3,)),
        dma((3,)), dma((3,)), dma, dma,
        dma((NCH, LEVELS, 3)), dma((NCH, LEVELS, 3)), dma((NCH, LEVELS, 3)), dma((NCH, LEVELS, 3)),
        dma((NCH, LEVELS)), dma((NCH, LEVELS)),
        dma((n, 2, 2)), dma((n, 2, 2)), dma((n, 2, 2)), dma((n, 2, 2)),
        dma((n, 2, 3)), dma((n, 2, 3)),
        dma((NCH,)), dma((NCH,)),
        dma((NCH, 2, 3)), dma((NCH, 2, 3)), dma((NCH, 2, 3)), dma((NCH, 2, 3)),
        dma((3,)), dma((3,)),
        dma((2, 3)), dma((2, 3)), dma((2, 3)), dma((2, 3)),
        dma, dma,
    ]
    in_vmem = pl.BlockSpec(memory_space=pltpu.VMEM)
    in_any = pl.BlockSpec(memory_space=pl.ANY)
    shapes = (
        jax.ShapeDtypeStruct((LEVELS, 64, D), F32),
        jax.ShapeDtypeStruct((2, 4, 4, 24, D), F32),
        jax.ShapeDtypeStruct((TOK, D), F32),
    )
    outs = pl.pallas_call(
        kernel,
        out_shape=shapes,
        in_specs=[in_any, in_any, in_any, in_vmem],
        out_specs=(in_any,) * 3,
        scratch_shapes=scratch,
        compiler_params=pltpu.CompilerParams(
            collective_id=0, has_side_effects=True, vmem_limit_bytes=62 * 2**20
        ),
        cost_estimate=pl.CostEstimate(flops=13 * 10**9, bytes_accessed=16 * 10**6, transcendentals=0),
        name="quantizer_step",
    )(hidden, enc_weight, codebook, codes)
    code_grad, enc_grad, last = pl.pallas_call(
        store,
        out_shape=shapes,
        in_specs=[in_any] * 3,
        out_specs=(in_any,) * 3,
        scratch_shapes=[vmem(o.shape, F32) for o in shapes] + [dma((6,)), dma((6,))],
        name="store",
    )(*outs)
    return code_grad[:, None], enc_grad.reshape(D, D), last


def solution(mesh):
    in_specs = (P(("items", "book"), None), P(), P(None, "book", None), P(None, ("items", "book")))
    out_specs = (P(None, "book", "items", None), P(), P(("items", "book"), None))
    return jax.shard_map(
        on_device, mesh=mesh, in_specs=in_specs, out_specs=out_specs, check_vma=False
    )
```

time: 579 us -> 106 us (0.18)
  waiting for transfers between devices: 501 us -> 0 us
  Pallas kernels: 0 us -> 105 us
  matrix products: 39 us -> 0 us
  between operations: 14.2 us -> 0.8 us
  blocking collectives: 12.8 us -> 0 us
  other arithmetic: 8.85 us -> 0 us
    reduce_scatter x4 -> x0, waiting for transfers between devices: 316 us -> none  [the longest x3 264 us: own_rows(): lax.psum_scatter(portion(jnp.int32(0), count), axis, scatter_dimension=0,...]
    psum x1 -> x0, waiting for transfers between devices: 134 us -> none  [on_device(): lax.psum(product, ('items', 'book'))]
    pallas_call x0 -> x2, Pallas kernels: none -> 105 us  [the longest x1 102 us: on_device(): pl.pallas_call(kernel, out_shape=shapes, in_specs=[in_any, in_any, in_any...]
    all_gather x1 -> x0, waiting for transfers between devices: 50.5 us -> none  [on_device(): group_grads = lax.all_gather(jnp.stack(grads), 'book', axis=1, tiled=True)]
    dot_general x8 -> x0, matrix products: 39 us -> none  [the longest x3 23.3 us: level_term(): lax.dot_general(hits, group_grads[level], (((0,), (0,)), ((), ())), prefe...]
    all_gather x1 -> x0, blocking collectives: 12.8 us -> none  [on_device(): group_codes = lax.all_gather(codes, 'book', axis=1, tiled=True)]
  transfers between devices with their start and end apart: 6 -> 0, of which waited for: 6 -> 0; matrix products, arithmetic and copies ran while one was open for 5% -> 0% of each run, Pallas kernels for 0% -> 0%
where the time goes in v2:
time: 106 us
  Pallas kernels  105 us (99%)
    pallas_call x1, Pallas kernels, on_device(): pl.pallas_call(kernel, out_shape=shapes, in_specs=[in_any, in_any, in_any...  102 us
    pallas_call x1, Pallas kernels, on_device(): pl.pallas_call(store, out_shape=shapes, in_specs=[in_any] * 3, out_specs=...  3.13 us

profile of v2, /device:TPU:0, one launch (start us, length us, event | category | flops | bytes accessed | tf_op | source)
XLA Modules:
  0.0 105.8 jit_solution(1542838664936789146)
XLA Ops:
  0.6 101.9 %quantizer_step.1 = (f32[3,64,768]{2,1,0:T(8,128)}, f32[2,4,4,24,768]{4,3,2,1,0:T(8,128)}, f32[256,768]{1,0:T(8,128)}) custom-call(bf16[256,768]{1,0:T(8,128)(2,1)} %hid_hbm.1, bf16[768,768]{1,0:T(8,128)(2,1)} %w_hbm.1, bf16[3,2048,768]{2,1,0:T(8,128)(2,1)} %cb_hbm.1, s32[3,256]{1,0:T(4,128)} %codes.1), custom_call_target="tpu_custom_call" | custom-call | flops 12999999488 | bytes 16000000 | tf_op jit(solution)/shard_map/quantizer_step/pallas_call | solution.py:482
  102.5 3.1 %store.1 = (f32[3,64,768]{2,1,0:T(8,128)}, f32[2,4,4,24,768]{4,3,2,1,0:T(8,128)}, f32[256,768]{1,0:T(8,128)}) custom-call(f32[3,64,768]{2,1,0:T(8,128)} %get-tuple-element.9.a_hbm, f32[2,4,4,24,768]{4,3,2,1,0:T(8,128)} %get-tuple-element.10.b_hbm, f32[256,768]{1,0:T(8,128)} %get-tuple-element.11.c_hbm), custom_call_target="tpu_custom_call" | custom-call | tf_op jit(solution)/shard_map/store/pallas_call | solution.py:494

commit v3 on v2

--- a/solution.py
+++ b/solution.py
@@ -72,6 +72,9 @@
     def wait(cps):
         for cp in cps:
             cp.wait()
+
+    def took(ref, sem):
+        pltpu.make_async_copy(ref, ref, sem).wait()
 
     bar = pltpu.get_barrier_semaphore()
     for k in (1, 2, 3):
@@ -111,14 +114,13 @@
     rc[0] = pk[0]
 
     pl.semaphore_wait(bar, 10)
-    pk_cp = start([
-        remote(pk.at[k], rc.at[4 - k], pk_ss.at[k - 1], pk_rs.at[k - 1], at_y(k)) for k in (2, 1, 3)
+    start([
+        remote(pk.at[k], rc.at[4 - k], pk_ss, pk_rs, at_y(k)) for k in (2, 1, 3)
     ])
     for l in range(LEVELS):
         ut[l] = onehot(iota((SLOTS, TOK), 0) == pos_i[l : l + 1, :])
-    wait(pk_cp)
-    rcs_cp = remote(rc, rcs, rcs_ss, rcs_rs, sib)
-    rcs_cp.start()
+    took(rc.at[1:4], pk_rs)
+    remote(rc, rcs, rcs_ss, rcs_rs, sib).start()
 
     held = jnp.concatenate([rc[k] for k in range(4)], axis=1)
     held_t = held.T.astype(I32)
@@ -127,7 +129,7 @@
         return [
             remote(
                 fs.at[ch, l, k - 1], rr.at[ch, l, 4 - k],
-                f_ss.at[ch, l, k - 1], f_rs.at[ch, l, k - 1], at_y(k),
+                f_ss, f_rs.at[ch], at_y(k),
             )
             for k in (2, 1, 3)
         ]
@@ -141,7 +143,6 @@
         for k in (1, 2, 3):
             fs[ch, l, k - 1] = got[k * CAP : (k + 1) * CAP]
 
-    f_cp = [[], [], []]
     for l in range(LEVELS):
         col = held_t[:, l : l + 1]
         for h in range(2):
@@ -150,21 +151,17 @@
             )
         cb_cp[l].wait()
         fetch(0, l)
-        f_cp[0] += start(fetch_copies(0, l))
+        start(fetch_copies(0, l))
     for ch in (1, 2):
         for l in range(LEVELS):
             fetch(ch, l)
-            f_cp[ch] += fetch_copies(ch, l)
             if ch == 1:
-                start(f_cp[1][-3:])
+                start(fetch_copies(1, l))
     wait(in_cp)
-
-    g_cp = {}
-    ec_cp = {}
 
     def chain(ch):
         cols = slice(ch * CW, (ch + 1) * CW)
-        wait(f_cp[ch])
+        took(rr.at[ch, :, 1:4], f_rs.at[ch])
         r = dot(hid[...], w[:, cols])
         res = []
         for l in range(LEVELS):
@@ -178,10 +175,10 @@
             gr[ch, l, 0] = packed[0:CAP]
             for k in (1, 2, 3):
                 gs[ch, l, k - 1] = packed[k * CAP : (k + 1) * CAP]
-            g_cp[ch, l] = start([
+            start([
                 remote(
                     gs.at[ch, l, k - 1], gr.at[ch, l, 4 - k],
-                    g_ss.at[ch, l, k - 1], g_rs.at[ch, l, k - 1], at_y(k),
+                    g_ss, g_rs.at[ch, l], at_y(k),
                 )
                 for k in (2, 1, 3)
             ])
@@ -190,31 +187,29 @@
             hid[...], cl, (((0,), (0,)), ((), ())), preferred_element_type=F32
         )
         e[ch] = prod.reshape(2, 4, 4, 24, CW)
-        ec_cp[ch] = start([
-            remote(e.at[ch, 1 - c], ec.at[ch], ec_ss.at[ch], ec_rs.at[ch], sib)
-        ])
-
-    e1_cp = {}
-    e2_cp = {}
+        remote(e.at[ch, 1 - c], ec.at[ch], ec_ss, ec_rs.at[ch], sib).start()
+
+    out_cp = []
+
     HW = CW // 2
 
     def enc_b(ch):
-        wait(ec_cp[ch])
+        took(ec.at[ch], ec_rs.at[ch])
         e[ch, c] = e[ch, c] + ec[ch]
         cps = []
         for k in (2, 1, 3):
             cps.append(remote(
                 e.at[ch, c, :, (x + k) % 4, :, 0:HW], e1r.at[ch, 0, k - 1],
-                e1_ss.at[ch, 0, k - 1], e1_rs.at[ch, 0, k - 1], at_x(k),
+                e1_ss, e1_rs.at[ch], at_x(k),
             ))
             cps.append(remote(
                 e.at[ch, c, (z + k) % 4, :, :, HW:CW], e1r.at[ch, 1, k - 1],
-                e1_ss.at[ch, 1, k - 1], e1_rs.at[ch, 1, k - 1], at_z(k),
+                e1_ss, e1_rs.at[ch], at_z(k),
             ))
-        e1_cp[ch] = start(cps)
+        start(cps)
 
     def enc_c(ch):
-        wait(e1_cp[ch])
+        took(e1r.at[ch], e1_rs.at[ch])
         t0 = e[ch, c, :, x, :, 0:HW]
         t1 = e[ch, c, z, :, :, HW:CW]
         for k in range(3):
@@ -226,38 +221,77 @@
         for k in (2, 1, 3):
             cps.append(remote(
                 e2s.at[ch, 0, (z + k) % 4], e2r.at[ch, 0, k - 1],
-                e2_ss.at[ch, 0, k - 1], e2_rs.at[ch, 0, k - 1], at_z(k),
+                e2_ss, e2_rs.at[ch], at_z(k),
             ))
             cps.append(remote(
                 e2s.at[ch, 1, (x + k) % 4], e2r.at[ch, 1, k - 1],
-                e2_ss.at[ch, 1, k - 1], e2_rs.at[ch, 1, k - 1], at_x(k),
+                e2_ss, e2_rs.at[ch], at_x(k),
             ))
-        e2_cp[ch] = start(cps)
+        start(cps)
 
     def enc_d(ch):
-        wait(e2_cp[ch])
+        took(e2r.at[ch], e2_rs.at[ch])
         t0 = e2s[ch, 0, z]
         t1 = e2s[ch, 1, x]
         for k in range(3):
             t0 = t0 + e2r[ch, 0, k]
             t1 = t1 + e2r[ch, 1, k]
-        ey[y, :, ch * CW : ch * CW + HW] = t0
-        ey[y, :, ch * CW + HW : (ch + 1) * CW] = t1
-
-    sib_cp, far_cp, near_cp, s2_cp, out_cp = {}, {}, {}, {}, []
+        ey[ch, y, :, 0:HW] = t0
+        ey[ch, y, :, HW:CW] = t1
+        start([
+            remote(ey.at[ch, y], ey.at[ch, y], ey_ss, ey_rs.at[ch], at_y(k)) for k in (2, 1, 3)
+        ])
+
+    def gather(ch, turn, ss, rs):
+        lo = slice(ch * CW, ch * CW + HW)
+        hi = slice(ch * CW + HW, (ch + 1) * CW)
+        cps = []
+        for k in (2, 1, 3):
+            if turn == 1:
+                va = enc_out.at[c, z, x, :, lo]
+                vb = enc_out.at[c, z, x, :, hi]
+                da, db = at_x(k), at_z(k)
+            else:
+                va = enc_out.at[c, z, :, :, lo]
+                vb = enc_out.at[c, :, x, :, hi]
+                da, db = at_z(k), at_x(k)
+            cps.append(remote(va, va, ss, rs.at[ch], da))
+            cps.append(remote(vb, vb, ss, rs.at[ch], db))
+        start(cps)
+
+    def enc_e(ch):
+        took(ey.at[ch, 0:3], ey_rs.at[ch])
+        total = ((ey[ch, 0] + ey[ch, 1]) + ey[ch, 2]) + ey[ch, 3]
+        enc_out[c, z, x, :, ch * CW : (ch + 1) * CW] = total * (1.0 / (TOK * 128))
+        gather(ch, 1, a1_ss, a1_rs)
+
+    def enc_f(ch):
+        took(ey.at[ch, 0:3], a1_rs.at[ch])
+        gather(ch, 2, a2_ss, a2_rs)
+
+    def enc_g(ch):
+        took(ec.at[ch, 0:3], a2_rs.at[ch])
+        part = enc_out.at[c, :, :, :, ch * CW : (ch + 1) * CW]
+        remote(part, part, a3_ss, a3_rs.at[ch], sib).start()
+
+    def enc_h(ch):
+        cols = slice(ch * CW, (ch + 1) * CW)
+        took(enc_out.at[1 - c, :, :, :, cols], a3_rs.at[ch])
+        out_cp.extend(start([pltpu.make_async_copy(
+            enc_out.at[:, :, :, :, cols], enc_hbm.at[:, :, :, :, cols], out_sem.at[1 + ch]
+        )]))
+
 
     def unit_a(n):
         ch, l = UNITS[n]
-        wait(g_cp[ch, l])
-        sib_cp[n] = start([
-            remote(gr.at[ch, l], gsib.at[ch, l], sib_ss.at[ch, l], sib_rs.at[ch, l], sib)
-        ])
+        took(gr.at[ch, l, 1:4], g_rs.at[ch, l])
+        remote(gr.at[ch, l], gsib.at[ch, l], sib_ss, sib_rs.at[ch, l], sib).start()
 
     def unit_b(n):
         ch, l = UNITS[n]
         q = n % RING
         acc = dot(oh[l, :, 0:SLOTS], gr[ch, l].reshape(SLOTS, CW))
-        wait(sib_cp[n])
+        took(gsib.at[ch, l], sib_rs.at[ch, l])
         acc = acc + dot(oh[l, :, SLOTS:], gsib[ch, l].reshape(SLOTS, CW))
         dd[q] = acc.reshape(4, 4, 64, CW)
         x2 = (x + 2) % 4
@@ -269,13 +303,13 @@
             for h, at in enumerate((at_x, at_z)):
                 cps.append(remote(
                     fars.at[n, h, d], farr.at[n, h, d],
-                    far_ss.at[n, h, d], far_rs.at[n, h, d], at(k),
+                    far_ss, far_rs.at[n], at(k),
                 ))
-        far_cp[n] = start(cps)
+        start(cps)
 
     def unit_c(n):
         q = n % RING
-        wait(far_cp[n])
+        took(farr.at[n], far_rs.at[n])
         cps = []
         for d, k in enumerate((1, 3)):
             xk = (x + k) % 4
@@ -292,13 +326,13 @@
             for h, at in enumerate((at_x, at_z)):
                 cps.append(remote(
                     nears.at[n, h, d], nearr.at[n, h, d],
-                    near_ss.at[n, h, d], near_rs.at[n, h, d], at(k),
+                    near_ss, near_rs.at[n], at(k),
                 ))
-        near_cp[n] = start(cps)
+        start(cps)
 
     def unit_d(n):
         q = n % RING
-        wait(near_cp[n])
+        took(nearr.at[n], near_rs.at[n])
         tx = dd[q, :, x, 0:32, :]
         tz = dd[q, z, :, 32:64, :]
         for d in range(2):
@@ -310,18 +344,18 @@
         for k in (2, 1, 3):
             cps.append(remote(
                 s2s.at[n, 0, (z + k) % 4], s2r.at[n, 0, k - 1],
-                s2_ss.at[n, 0, k - 1], s2_rs.at[n, 0, k - 1], at_z(k),
+                s2_ss, s2_rs.at[n], at_z(k),
             ))
             cps.append(remote(
                 s2s.at[n, 1, (x + k) % 4], s2r.at[n, 1, k - 1],
-                s2_ss.at[n, 1, k - 1], s2_rs.at[n, 1, k - 1], at_x(k),
+                s2_ss, s2_rs.at[n], at_x(k),
             ))
-        s2_cp[n] = start(cps)
+        start(cps)
 
     def unit_e(n):
         ch, l = UNITS[n]
         cols = slice(ch * CW, (ch + 1) * CW)
-        wait(s2_cp[n])
+        took(s2r.at[n], s2_rs.at[n])
         t0 = s2s[n, 0, z]
         t1 = s2s[n, 1, x]
         for k in range(3):
@@ -330,79 +364,105 @@
         cg_out[l, 0:32, cols] = -t0
         cg_out[l, 32:64, cols] = -t1
 
-    def step(t):
-        for lag, op in enumerate((unit_a, unit_b, unit_c, unit_d, unit_e)):
-            if 0 <= t - lag < len(UNITS):
-                op(t - lag)
-
-    H = D // 2
-
-    def gather(turn, ss, rs):
-        cps = []
-        for k in (2, 1, 3):
-            if turn == 1:
-                va = enc_out.at[c, z, x, :, 0:H]
-                vb = enc_out.at[c, z, x, :, H:D]
-                da, db = at_x(k), at_z(k)
-            else:
-                va = enc_out.at[c, z, :, :, 0:H]
-                vb = enc_out.at[c, :, x, :, H:D]
-                da, db = at_z(k), at_x(k)
-            cps.append(remote(va, va, ss.at[0, k - 1], rs.at[0, k - 1], da))
-            cps.append(remote(vb, vb, ss.at[1, k - 1], rs.at[1, k - 1], db))
-        return start(cps)
-
+    def code_store(ch):
+        cols = slice(ch * CW, (ch + 1) * CW)
+        out_cp.extend(start([pltpu.make_async_copy(
+            cg_out.at[:, :, cols], cg_hbm.at[:, :, cols], out_sem.at[4 + ch]
+        )]))
+
+    def own_codes():
+        took(rcs, rcs_rs)
+        for l in range(LEVELS):
+            for h, src in enumerate((rc, rcs)):
+                slot_code = jnp.concatenate(
+                    [src[k, l : l + 1, :] for k in range(4)], axis=1
+                ).astype(I32)
+                rows = iota((1024, SLOTS), 0)
+                code = ((rows >> 6) << 7) + c * 64 + (rows & 63) + 1
+                oh[l, :, h * SLOTS : (h + 1) * SLOTS] = onehot(code == slot_code)
+
+    own_codes()
     chain(0)
-    rcs_cp.wait()
+    enc_b(0)
+    enc_c(0)
+    chain(1)
     for l in range(LEVELS):
-        for h, src in enumerate((rc, rcs)):
-            slot_code = jnp.concatenate(
-                [src[k, l : l + 1, :] for k in range(4)], axis=1
-            ).astype(I32)
-            rows = iota((1024, SLOTS), 0)
-            code = ((rows >> 6) << 7) + c * 64 + (rows & 63) + 1
-            oh[l, :, h * SLOTS : (h + 1) * SLOTS] = onehot(code == slot_code)
-    enc_b(0)
-    wait(f_cp[1])
-    start(f_cp[2])
-    f_cp[1] = []
-    chain(1)
-    enc_c(0)
+        start(fetch_copies(2, l))
+    enc_d(0)
+    unit_a(0)
     enc_b(1)
-    step(0)
-    enc_d(0)
+    unit_b(0)
+    unit_a(1)
+    unit_b(1)
+    unit_c(0)
     enc_c(1)
-    step(1)
+    unit_a(2)
+    unit_b(2)
+    unit_c(1)
+    unit_a(3)
+    unit_d(0)
+    unit_b(3)
+    unit_a(4)
     enc_d(1)
-    step(2)
+    unit_c(2)
+    unit_d(1)
+    unit_b(4)
+    unit_c(3)
+    unit_a(5)
+    unit_e(0)
+    unit_b(5)
+    unit_e(1)
+    unit_c(4)
+    unit_d(2)
+    unit_c(5)
+    unit_d(3)
+    unit_d(4)
     chain(2)
     out_cp += start([pltpu.make_async_copy(res_out, res_hbm, out_sem.at[0])])
-    step(3)
+    enc_e(0)
+    unit_e(2)
+    code_store(0)
+    unit_d(5)
     enc_b(2)
-    step(4)
+    enc_e(1)
+    unit_e(3)
+    enc_f(0)
+    unit_e(4)
+    unit_a(6)
+    unit_e(5)
+    code_store(1)
+    unit_b(6)
     enc_c(2)
-    step(5)
+    unit_a(7)
+    enc_f(1)
+    unit_b(7)
+    unit_a(8)
+    unit_c(6)
     enc_d(2)
-    ey_cp = start([
-        remote(ey.at[y], ey.at[y], ey_ss.at[k - 1], ey_rs.at[k - 1], at_y(k)) for k in (2, 1, 3)
-    ])
-    step(6)
-    wait(ey_cp)
-    enc_out[c, z, x] = (((ey[0] + ey[1]) + ey[2]) + ey[3]) * (1.0 / (TOK * 128))
-    a1_cp = gather(1, a1_ss, a1_rs)
-    step(7)
-    wait(a1_cp)
-    a2_cp = gather(2, a2_ss, a2_rs)
-    step(8)
-    step(9)
-    wait(a2_cp)
-    a3_cp = start([remote(enc_out.at[c], enc_out.at[c], a3_ss, a3_rs, sib)])
-    step(10)
-    wait(a3_cp)
-    out_cp += start([pltpu.make_async_copy(enc_out, enc_hbm, out_sem.at[1])])
-    step(11)
-    step(12)
-    out_cp += start([pltpu.make_async_copy(cg_out, cg_hbm, out_sem.at[2])])
+    unit_b(8)
+    enc_g(1)
+    unit_c(7)
+    enc_e(2)
+    unit_d(6)
+    unit_c(8)
+    enc_h(1)
+    enc_g(0)
+    enc_h(0)
+    enc_f(2)
+    unit_d(7)
+    unit_e(6)
+    unit_d(8)
+    enc_g(2)
+    unit_e(7)
+    enc_h(2)
+    unit_e(8)
+    code_store(2)
+    for ref, sem in (
+        (pk.at[1:4], pk_ss), (rc, rcs_ss), (fs, f_ss), (gs, g_ss), (gr, sib_ss), (fars, far_ss),
+        (nears, near_ss), (s2r, s2_ss), (ec, ec_ss), (e1r, e1_ss), (e2r, e2_ss), (ey.at[:, 0:3], ey_ss),
+        (ey.at[:, 0:3], a1_ss), (ec.at[:, 0:3], a2_ss), (ec, a3_ss),
+    ):
+        took(ref, sem)
     wait(out_cp)
 
 
@@ -456,21 +516,16 @@
         vmem((NCH, 2, 3, 4, 24, CW // 2), F32),
         vmem((NCH, 2, 4, 24, CW // 2), F32),
         vmem((NCH, 2, 3, 24, CW // 2), F32),
-        vmem((4, 24, D), F32),
+        vmem((NCH, 4, 24, CW), F32),
         vmem((LEVELS, 64, D), F32),
         vmem((2, 4, 4, 24, D), F32),
         vmem((TOK, D), F32),
-        dma((2,)), dma((LEVELS,)), dma((3,)),
-        dma((3,)), dma((3,)), dma, dma,
-        dma((NCH, LEVELS, 3)), dma((NCH, LEVELS, 3)), dma((NCH, LEVELS, 3)), dma((NCH, LEVELS, 3)),
-        dma((NCH, LEVELS)), dma((NCH, LEVELS)),
-        dma((n, 2, 2)), dma((n, 2, 2)), dma((n, 2, 2)), dma((n, 2, 2)),
-        dma((n, 2, 3)), dma((n, 2, 3)),
-        dma((NCH,)), dma((NCH,)),
-        dma((NCH, 2, 3)), dma((NCH, 2, 3)), dma((NCH, 2, 3)), dma((NCH, 2, 3)),
-        dma((3,)), dma((3,)),
-        dma((2, 3)), dma((2, 3)), dma((2, 3)), dma((2, 3)),
-        dma, dma,
+        dma((2,)), dma((LEVELS,)), dma((1 + 2 * NCH,)),
+        dma, dma, dma, dma,
+        dma, dma((NCH,)), dma, dma((NCH, LEVELS)), dma, dma((NCH, LEVELS)),
+        dma, dma((n,)), dma, dma((n,)), dma, dma((n,)),
+        dma, dma((NCH,)), dma, dma((NCH,)), dma, dma((NCH,)),
+        dma, dma((NCH,)), dma, dma((NCH,)), dma, dma((NCH,)), dma, dma((NCH,)),
     ]
     in_vmem = pl.BlockSpec(memory_space=pltpu.VMEM)
     in_any = pl.BlockSpec(memory_space=pl.ANY)

time: 106 us -> 95.8 us (0.904); the launches traced: 106 us -> 94.1 us
  Pallas kernels: 105 us -> 93.3 us
    pallas_call x1, Pallas kernels: 102 us -> 90.2 us  [on_device(): pl.pallas_call(kernel, out_shape=shapes, in_specs=[in_any, in_any, in_any...]
where the time goes in v3:
time: 95.8 us; the launch traced here: 94.1 us
  Pallas kernels  93.3 us (97%)
    pallas_call x1, Pallas kernels, on_device(): pl.pallas_call(kernel, out_shape=shapes, in_specs=[in_any, in_any, in_any...  90.2 us
    pallas_call x1, Pallas kernels, on_device(): pl.pallas_call(store, out_shape=shapes, in_specs=[in_any] * 3, out_specs=...  3.13 us

profile of v3, /device:TPU:0, one launch (start us, length us, event | category | flops | bytes accessed | tf_op | source)
XLA Modules:
  0.0 94.1 jit_solution(17020460489858975953)
XLA Ops:
  0.6 90.2 %quantizer_step.1 = (f32[3,64,768]{2,1,0:T(8,128)}, f32[2,4,4,24,768]{4,3,2,1,0:T(8,128)}, f32[256,768]{1,0:T(8,128)}) custom-call(bf16[256,768]{1,0:T(8,128)(2,1)} %hid_hbm.1, bf16[768,768]{1,0:T(8,128)(2,1)} %w_hbm.1, bf16[3,2048,768]{2,1,0:T(8,128)(2,1)} %cb_hbm.1, s32[3,256]{1,0:T(4,128)} %codes.1), custom_call_target="tpu_custom_call" | custom-call | flops 12999999488 | bytes 16000000 | tf_op jit(solution)/shard_map/quantizer_step/pallas_call | solution.py:537
  90.9 3.1 %store.1 = (f32[3,64,768]{2,1,0:T(8,128)}, f32[2,4,4,24,768]{4,3,2,1,0:T(8,128)}, f32[256,768]{1,0:T(8,128)}) custom-call(f32[3,64,768]{2,1,0:T(8,128)} %get-tuple-element.9.a_hbm, f32[2,4,4,24,768]{4,3,2,1,0:T(8,128)} %get-tuple-element.10.b_hbm, f32[256,768]{1,0:T(8,128)} %get-tuple-element.11.c_hbm), custom_call_target="tpu_custom_call" | custom-call | tf_op jit(solution)/shard_map/store/pallas_call | solution.py:549

commit v4 on v3

--- a/solution.py
+++ b/solution.py
@@ -35,10 +35,10 @@
 
 
 def kernel(
-    hid_hbm, w_hbm, cb_hbm, codes, cg_hbm, enc_hbm, res_hbm,
+    hid_hbm, w_hbm, cb_hbm, codes, cg_out, enc_out, res_out,
     hid, w, cb, code8, pk, rc, rcs, ut, u, oh, fs, rr, gs, gr, gsib, dd,
-    fars, farr, nears, nearr, s2s, s2r, e, ec, e1r, e2s, e2r, ey, cg_out, enc_out, res_out,
-    in_sem, cb_sem, out_sem, pk_ss, pk_rs, rcs_ss, rcs_rs, f_ss, f_rs, g_ss, g_rs, sib_ss, sib_rs,
+    fars, farr, nears, nearr, s2s, s2r, e, ec, e1r, e2s, e2r, ey,
+    in_sem, cb_sem, pk_ss, pk_rs, rcs_ss, rcs_rs, f_ss, f_rs, g_ss, g_rs, sib_ss, sib_rs,
     far_ss, far_rs, near_ss, near_rs, s2_ss, s2_rs, ec_ss, ec_rs, e1_ss, e1_rs, e2_ss, e2_rs,
     ey_ss, ey_rs, a1_ss, a1_rs, a2_ss, a2_rs, a3_ss, a3_rs,
 ):
@@ -182,14 +182,15 @@
                 )
                 for k in (2, 1, 3)
             ])
+            if (ch, l) == (1, 1):
+                for fl in range(LEVELS):
+                    start(fetch_copies(2, fl))
         res_out[:, cols] = r
         prod = lax.dot_general(
             hid[...], cl, (((0,), (0,)), ((), ())), preferred_element_type=F32
         )
         e[ch] = prod.reshape(2, 4, 4, 24, CW)
         remote(e.at[ch, 1 - c], ec.at[ch], ec_ss, ec_rs.at[ch], sib).start()
-
-    out_cp = []
 
     HW = CW // 2
 
@@ -277,9 +278,6 @@
     def enc_h(ch):
         cols = slice(ch * CW, (ch + 1) * CW)
         took(enc_out.at[1 - c, :, :, :, cols], a3_rs.at[ch])
-        out_cp.extend(start([pltpu.make_async_copy(
-            enc_out.at[:, :, :, :, cols], enc_hbm.at[:, :, :, :, cols], out_sem.at[1 + ch]
-        )]))
 
 
     def unit_a(n):
@@ -364,12 +362,6 @@
         cg_out[l, 0:32, cols] = -t0
         cg_out[l, 32:64, cols] = -t1
 
-    def code_store(ch):
-        cols = slice(ch * CW, (ch + 1) * CW)
-        out_cp.extend(start([pltpu.make_async_copy(
-            cg_out.at[:, :, cols], cg_hbm.at[:, :, cols], out_sem.at[4 + ch]
-        )]))
-
     def own_codes():
         took(rcs, rcs_rs)
         for l in range(LEVELS):
@@ -386,68 +378,63 @@
     enc_b(0)
     enc_c(0)
     chain(1)
-    for l in range(LEVELS):
-        start(fetch_copies(2, l))
+    unit_a(0)
     enc_d(0)
-    unit_a(0)
     enc_b(1)
     unit_b(0)
     unit_a(1)
     unit_b(1)
+    unit_a(2)
+    enc_c(1)
+    unit_b(2)
     unit_c(0)
-    enc_c(1)
-    unit_a(2)
-    unit_b(2)
+    unit_a(3)
     unit_c(1)
-    unit_a(3)
-    unit_d(0)
     unit_b(3)
-    unit_a(4)
     enc_d(1)
     unit_c(2)
+    unit_a(4)
+    unit_d(0)
+    unit_b(4)
     unit_d(1)
-    unit_b(4)
     unit_c(3)
+    unit_d(2)
+    unit_e(0)
+    unit_c(4)
+    chain(2)
+    unit_d(3)
+    unit_e(1)
     unit_a(5)
-    unit_e(0)
+    enc_b(2)
+    unit_e(2)
+    enc_e(0)
+    unit_d(4)
     unit_b(5)
-    unit_e(1)
-    unit_c(4)
-    unit_d(2)
-    unit_c(5)
-    unit_d(3)
-    unit_d(4)
-    chain(2)
-    out_cp += start([pltpu.make_async_copy(res_out, res_hbm, out_sem.at[0])])
-    enc_e(0)
-    unit_e(2)
-    code_store(0)
-    unit_d(5)
-    enc_b(2)
     enc_e(1)
     unit_e(3)
+    unit_a(6)
+    enc_c(2)
     enc_f(0)
+    unit_b(6)
     unit_e(4)
-    unit_a(6)
-    unit_e(5)
-    code_store(1)
-    unit_b(6)
-    enc_c(2)
     unit_a(7)
+    unit_c(5)
     enc_f(1)
     unit_b(7)
+    enc_d(2)
     unit_a(8)
+    enc_g(0)
     unit_c(6)
-    enc_d(2)
     unit_b(8)
+    unit_d(5)
+    enc_h(0)
+    enc_e(2)
     enc_g(1)
     unit_c(7)
-    enc_e(2)
     unit_d(6)
+    enc_h(1)
     unit_c(8)
-    enc_h(1)
-    enc_g(0)
-    enc_h(0)
+    unit_e(5)
     enc_f(2)
     unit_d(7)
     unit_e(6)
@@ -456,31 +443,20 @@
     unit_e(7)
     enc_h(2)
     unit_e(8)
-    code_store(2)
     for ref, sem in (
         (pk.at[1:4], pk_ss), (rc, rcs_ss), (fs, f_ss), (gs, g_ss), (gr, sib_ss), (fars, far_ss),
         (nears, near_ss), (s2r, s2_ss), (ec, ec_ss), (e1r, e1_ss), (e2r, e2_ss), (ey.at[:, 0:3], ey_ss),
         (ey.at[:, 0:3], a1_ss), (ec.at[:, 0:3], a2_ss), (ec, a3_ss),
     ):
         took(ref, sem)
-    wait(out_cp)
-
-
-def store(a_hbm, b_hbm, c_hbm, ao, bo, co, av, bv, cv, in_sem, out_sem):
-    pieces = []
-    for k in range(2):
-        for q in range(2):
-            part = (k, pl.ds(2 * q, 2))
-            pieces.append((b_hbm.at[part], bv.at[part], bo.at[part]))
-    pieces += [(a_hbm, av, ao), (c_hbm, cv, co)]
-    loads = [pltpu.make_async_copy(s, v, in_sem.at[n]) for n, (s, v, o) in enumerate(pieces)]
-    stores = [pltpu.make_async_copy(v, o, out_sem.at[n]) for n, (s, v, o) in enumerate(pieces)]
-    for cp in loads:
+
+
+def store(a, b, c, ao, bo, co, sem):
+    cps = [pltpu.make_async_copy(b.at[k], bo.at[k], sem.at[k]) for k in range(2)]
+    cps += [pltpu.make_async_copy(a, ao, sem.at[2]), pltpu.make_async_copy(c, co, sem.at[3])]
+    for cp in cps:
         cp.start()
-    for load, back in zip(loads, stores):
-        load.wait()
-        back.start()
-    for cp in stores:
+    for cp in cps:
         cp.wait()
 
 
@@ -517,10 +493,7 @@
         vmem((NCH, 2, 4, 24, CW // 2), F32),
         vmem((NCH, 2, 3, 24, CW // 2), F32),
         vmem((NCH, 4, 24, CW), F32),
-        vmem((LEVELS, 64, D), F32),
-        vmem((2, 4, 4, 24, D), F32),
-        vmem((TOK, D), F32),
-        dma((2,)), dma((LEVELS,)), dma((1 + 2 * NCH,)),
+        dma((2,)), dma((LEVELS,)),
         dma, dma, dma, dma,
         dma, dma((NCH,)), dma, dma((NCH, LEVELS)), dma, dma((NCH, LEVELS)),
         dma, dma((n,)), dma, dma((n,)), dma, dma((n,)),
@@ -536,24 +509,17 @@
     )
     outs = pl.pallas_call(
         kernel,
-        out_shape=shapes,
+        out_shape=tuple(pltpu.VMEM(o.shape, F32) for o in shapes),
         in_specs=[in_any, in_any, in_any, in_vmem],
-        out_specs=(in_any,) * 3,
+        out_specs=(in_vmem,) * 3,
         scratch_shapes=scratch,
         compiler_params=pltpu.CompilerParams(
-            collective_id=0, has_side_effects=True, vmem_limit_bytes=62 * 2**20
+            collective_id=0, has_side_effects=True, vmem_limit_bytes=58 * 2**20
         ),
         cost_estimate=pl.CostEstimate(flops=13 * 10**9, bytes_accessed=16 * 10**6, transcendentals=0),
         name="quantizer_step",
     )(hidden, enc_weight, codebook, codes)
-    code_grad, enc_grad, last = pl.pallas_call(
-        store,
-        out_shape=shapes,
-        in_specs=[in_any] * 3,
-        out_specs=(in_any,) * 3,
-        scratch_shapes=[vmem(o.shape, F32) for o in shapes] + [dma((6,)), dma((6,))],
-        name="store",
-    )(*outs)
+    code_grad, enc_grad, last = outs
     return code_grad[:, None], enc_grad.reshape(D, D), last
 
 

time: 95.8 us -> 93.5 us (0.976); the launches traced: 94.1 us -> 93.1 us
  Pallas kernels: 93.3 us -> 89.4 us
  local copies, waits for them, and re-layouts: 0 us -> 3.1 us
    pallas_call x2 -> x1, Pallas kernels: 93.3 us -> 89.4 us  [on_device(): pl.pallas_call(kernel, out_shape=tuple((pltpu.VMEM(o.shape, F32) for o in...]
    unnamed x0 -> x3, local copies, waits for them, and re-layouts: none -> 3.1 us
where the time goes in v4:
time: 93.5 us; the launch traced here: 93.1 us
  Pallas kernels  89.4 us (96%)
  local copies, waits for them, and re-layouts  3.1 us (3%)
    pallas_call x1, Pallas kernels, on_device(): pl.pallas_call(kernel, out_shape=tuple((pltpu.VMEM(o.shape, F32) for o in...  89.4 us
    unnamed x3, local copies, waits for them, and re-layouts  3.1 us

profile of v4, /device:TPU:0, one launch (start us, length us, event | category | flops | bytes accessed | tf_op | source)
XLA Modules:
  0.0 93.1 jit_solution(17847180864030690601)
XLA Ops:
  0.6 89.4 %quantizer_step.1 = (f32[3,64,768]{2,1,0:T(8,128)S(1)}, f32[2,4,4,24,768]{4,3,2,1,0:T(8,128)S(1)}, f32[256,768]{1,0:T(8,128)S(1)}) custom-call(bf16[256,768]{1,0:T(8,128)(2,1)} %hid_hbm.1, bf16[768,768]{1,0:T(8,128)(2,1)} %w_hbm.1, bf16[3,2048,768]{2,1,0:T(8,128)(2,1)} %cb_hbm.1, s32[3,256]{1,0:T(4,128)} %codes.1), custom_call_target="tpu_custom_call" | custom-call | flops 12999999488 | bytes 16000000 | tf_op jit(solution)/shard_map/quantizer_step/pallas_call | solution.py:510
  90.0 0.8 copy.11
  90.8 1.4 %copy.12 = f32[768,768]{1,0:T(8,128)} copy(f32[768,768]{1,0:T(8,128)S(1)} %bitcast.4) | data formatting | bytes 4718592
  92.2 0.9 copy.13

commit v5 on v4

--- a/solution.py
+++ b/solution.py
@@ -20,6 +20,7 @@
 NCH = D // CW
 UNITS = [(ch, l) for ch in range(NCH) for l in (2, 1, 0)]
 RING = 6
+MERGED = 9
 
 
 def onehot(mask):
@@ -39,7 +40,7 @@
     hid, w, cb, code8, pk, rc, rcs, ut, u, oh, fs, rr, gs, gr, gsib, dd,
     fars, farr, nears, nearr, s2s, s2r, e, ec, e1r, e2s, e2r, ey,
     in_sem, cb_sem, pk_ss, pk_rs, rcs_ss, rcs_rs, f_ss, f_rs, g_ss, g_rs, sib_ss, sib_rs,
-    far_ss, far_rs, near_ss, near_rs, s2_ss, s2_rs, ec_ss, ec_rs, e1_ss, e1_rs, e2_ss, e2_rs,
+    far_ss, far_rs, near_ss, near_rs, s2_ss, s2_rs, h_ss, h_rs, m_ss, ec_ss, ec_rs, e1_ss, e1_rs, e2_ss, e2_rs,
     ey_ss, ey_rs, a1_ss, a1_rs, a2_ss, a2_rs, a3_ss, a3_rs,
 ):
     i = lax.axis_index("items")
@@ -129,7 +130,7 @@
         return [
             remote(
                 fs.at[ch, l, k - 1], rr.at[ch, l, 4 - k],
-                f_ss, f_rs.at[ch], at_y(k),
+                f_ss, f_rs.at[NCH + l if ch == 0 and l < 2 else ch], at_y(k),
             )
             for k in (2, 1, 3)
         ]
@@ -155,13 +156,18 @@
     for ch in (1, 2):
         for l in range(LEVELS):
             fetch(ch, l)
-            if ch == 1:
-                start(fetch_copies(1, l))
     wait(in_cp)
+    took(rr.at[0, 0, 1:4], f_rs.at[NCH])
+    for l in range(LEVELS):
+        start(fetch_copies(1, l))
 
     def chain(ch):
         cols = slice(ch * CW, (ch + 1) * CW)
-        took(rr.at[ch, :, 1:4], f_rs.at[ch])
+        if ch == 0:
+            took(rr.at[0, 1, 1:4], f_rs.at[NCH + 1])
+            took(rr.at[0, 2, 1:4], f_rs.at[0])
+        else:
+            took(rr.at[ch, :, 1:4], f_rs.at[ch])
         r = dot(hid[...], w[:, cols])
         res = []
         for l in range(LEVELS):
@@ -339,6 +345,17 @@
         s2s[n, 0] = tx
         s2s[n, 1] = tz
         cps = []
+        if n < MERGED:
+            for d, k in enumerate((1, 3)):
+                rows = pl.ds(16 * d, 16)
+                cps.append(remote(
+                    s2s.at[n, 0, (z + 2) % 4, rows], s2r.at[n, 0, 2, rows], h_ss, h_rs.at[n], at_z(k),
+                ))
+                cps.append(remote(
+                    s2s.at[n, 1, (x + 2) % 4, rows], s2r.at[n, 1, 2, rows], h_ss, h_rs.at[n], at_x(k),
+                ))
+            start(cps)
+            return
         for k in (2, 1, 3):
             cps.append(remote(
                 s2s.at[n, 0, (z + k) % 4], s2r.at[n, 0, k - 1],
@@ -350,13 +367,27 @@
             ))
         start(cps)
 
+    def unit_m(n):
+        took(s2r.at[n, :, 2], h_rs.at[n])
+        cps = []
+        for d, k in enumerate((1, 3)):
+            rows = slice(16 * d, 16 * d + 16)
+            zk = (z + k) % 4
+            xk = (x + k) % 4
+            s2s[n, 0, zk, rows] = s2s[n, 0, zk, rows] + s2r[n, 0, 2, rows]
+            s2s[n, 1, xk, rows] = s2s[n, 1, xk, rows] + s2r[n, 1, 2, rows]
+            cps.append(remote(s2s.at[n, 0, zk], s2r.at[n, 0, d], m_ss, s2_rs.at[n], at_z(k)))
+            cps.append(remote(s2s.at[n, 1, xk], s2r.at[n, 1, d], m_ss, s2_rs.at[n], at_x(k)))
+        start(cps)
+
     def unit_e(n):
         ch, l = UNITS[n]
         cols = slice(ch * CW, (ch + 1) * CW)
-        took(s2r.at[n], s2_rs.at[n])
+        parts = 2 if n < MERGED else 3
+        took(s2r.at[n, :, 0:parts], s2_rs.at[n])
         t0 = s2s[n, 0, z]
         t1 = s2s[n, 1, x]
-        for k in range(3):
+        for k in range(parts):
             t0 = t0 + s2r[n, 0, k]
             t1 = t1 + s2r[n, 1, k]
         cg_out[l, 0:32, cols] = -t0
@@ -376,76 +407,86 @@
     own_codes()
     chain(0)
     enc_b(0)
+    chain(1)
     enc_c(0)
-    chain(1)
     unit_a(0)
-    enc_d(0)
     enc_b(1)
     unit_b(0)
     unit_a(1)
+    enc_d(0)
     unit_b(1)
     unit_a(2)
     enc_c(1)
+    unit_c(0)
     unit_b(2)
-    unit_c(0)
     unit_a(3)
     unit_c(1)
     unit_b(3)
+    unit_d(0)
+    unit_a(4)
+    unit_c(2)
     enc_d(1)
-    unit_c(2)
-    unit_a(4)
-    unit_d(0)
     unit_b(4)
+    unit_c(3)
+    unit_m(0)
     unit_d(1)
-    unit_c(3)
     unit_d(2)
+    unit_c(4)
+    unit_d(3)
     unit_e(0)
-    unit_c(4)
+    unit_m(1)
     chain(2)
-    unit_d(3)
+    unit_m(2)
+    unit_m(3)
+    unit_d(4)
+    unit_a(5)
     unit_e(1)
-    unit_a(5)
     enc_b(2)
+    enc_e(0)
+    unit_b(5)
     unit_e(2)
-    enc_e(0)
-    unit_d(4)
-    unit_b(5)
+    unit_e(3)
+    unit_m(4)
     enc_e(1)
-    unit_e(3)
     unit_a(6)
     enc_c(2)
     enc_f(0)
     unit_b(6)
+    unit_a(7)
+    enc_f(1)
     unit_e(4)
-    unit_a(7)
     unit_c(5)
-    enc_f(1)
     unit_b(7)
     enc_d(2)
     unit_a(8)
     enc_g(0)
+    unit_b(8)
     unit_c(6)
-    unit_b(8)
+    enc_h(0)
+    enc_g(1)
+    enc_e(2)
     unit_d(5)
-    enc_h(0)
-    enc_e(2)
-    enc_g(1)
     unit_c(7)
-    unit_d(6)
     enc_h(1)
     unit_c(8)
+    unit_d(6)
+    enc_f(2)
+    unit_m(5)
+    unit_d(7)
+    unit_d(8)
+    unit_m(6)
+    enc_g(2)
+    unit_m(7)
+    unit_m(8)
     unit_e(5)
-    enc_f(2)
-    unit_d(7)
     unit_e(6)
-    unit_d(8)
-    enc_g(2)
+    enc_h(2)
     unit_e(7)
-    enc_h(2)
     unit_e(8)
     for ref, sem in (
         (pk.at[1:4], pk_ss), (rc, rcs_ss), (fs, f_ss), (gs, g_ss), (gr, sib_ss), (fars, far_ss),
-        (nears, near_ss), (s2r, s2_ss), (ec, ec_ss), (e1r, e1_ss), (e2r, e2_ss), (ey.at[:, 0:3], ey_ss),
+        (nears, near_ss), (s2r.at[0:MERGED, :, 2], h_ss), (s2r.at[0:MERGED, :, 0:2], m_ss),
+         (ec, ec_ss), (e1r, e1_ss), (e2r, e2_ss), (ey.at[:, 0:3], ey_ss),
         (ey.at[:, 0:3], a1_ss), (ec.at[:, 0:3], a2_ss), (ec, a3_ss),
     ):
         took(ref, sem)
@@ -495,8 +536,8 @@
         vmem((NCH, 4, 24, CW), F32),
         dma((2,)), dma((LEVELS,)),
         dma, dma, dma, dma,
-        dma, dma((NCH,)), dma, dma((NCH, LEVELS)), dma, dma((NCH, LEVELS)),
-        dma, dma((n,)), dma, dma((n,)), dma, dma((n,)),
+        dma, dma((NCH + 2,)), dma, dma((NCH, LEVELS)), dma, dma((NCH, LEVELS)),
+        dma, dma((n,)), dma, dma((n,)), dma, dma((n,)), dma, dma((n,)), dma,
         dma, dma((NCH,)), dma, dma((NCH,)), dma, dma((NCH,)),
         dma, dma((NCH,)), dma, dma((NCH,)), dma, dma((NCH,)), dma, dma((NCH,)),
     ]

time: 93.5 us -> 93.1 us (level)
  no operation moved by 1% of the time
where the time goes in v5:
time: 93.1 us; the launch traced here: 92.9 us
  Pallas kernels  89.2 us (96%)
  local copies, waits for them, and re-layouts  3.1 us (3%)
    pallas_call x1, Pallas kernels, on_device(): pl.pallas_call(kernel, out_shape=tuple((pltpu.VMEM(o.shape, F32) for o in...  89.2 us
    unnamed x3, local copies, waits for them, and re-layouts  3.1 us

profile of v5, /device:TPU:0, one launch (start us, length us, event | category | flops | bytes accessed | tf_op | source)
XLA Modules:
  0.0 92.9 jit_solution(4418172468619554427)
XLA Ops:
  0.6 89.2 %quantizer_step.1 = (f32[3,64,768]{2,1,0:T(8,128)S(1)}, f32[2,4,4,24,768]{4,3,2,1,0:T(8,128)S(1)}, f32[256,768]{1,0:T(8,128)S(1)}) custom-call(bf16[256,768]{1,0:T(8,128)(2,1)} %hid_hbm.1, bf16[768,768]{1,0:T(8,128)(2,1)} %w_hbm.1, bf16[3,2048,768]{2,1,0:T(8,128)(2,1)} %cb_hbm.1, s32[3,256]{1,0:T(4,128)} %codes.1), custom_call_target="tpu_custom_call" | custom-call | flops 12999999488 | bytes 16000000 | tf_op jit(solution)/shard_map/quantizer_step/pallas_call | solution.py:551
  89.8 0.8 copy.11
  90.6 1.4 %copy.12 = f32[768,768]{1,0:T(8,128)} copy(f32[768,768]{1,0:T(8,128)S(1)} %bitcast.4) | data formatting | bytes 4718592
  92.0 0.9 copy.13

commit v6 on v5

--- a/solution.py
+++ b/solution.py
@@ -158,8 +158,14 @@
             fetch(ch, l)
     wait(in_cp)
     took(rr.at[0, 0, 1:4], f_rs.at[NCH])
-    for l in range(LEVELS):
-        start(fetch_copies(1, l))
+
+    def fetch_rest(ch):
+        start([
+            remote(fs.at[ch, :, k - 1], rr.at[ch, :, 4 - k], f_ss, f_rs.at[ch], at_y(k))
+            for k in (2, 1, 3)
+        ])
+
+    fetch_rest(1)
 
     def chain(ch):
         cols = slice(ch * CW, (ch + 1) * CW)
@@ -189,8 +195,7 @@
                 for k in (2, 1, 3)
             ])
             if (ch, l) == (1, 1):
-                for fl in range(LEVELS):
-                    start(fetch_copies(2, fl))
+                fetch_rest(2)
         res_out[:, cols] = r
         prod = lax.dot_general(
             hid[...], cl, (((0,), (0,)), ((), ())), preferred_element_type=F32

time: 93.1 us -> 94.3 us (1.013)
  Pallas kernels: 89.2 us -> 90.4 us
    pallas_call x1, Pallas kernels: 89.2 us -> 90.4 us  [on_device(): pl.pallas_call(kernel, out_shape=tuple((pltpu.VMEM(o.shape, F32) for o in...]
where the time goes in v6:
time: 94.3 us; the launch traced here: 94.1 us
  Pallas kernels  90.4 us (96%)
  local copies, waits for them, and re-layouts  3.1 us (3%)
    pallas_call x1, Pallas kernels, on_device(): pl.pallas_call(kernel, out_shape=tuple((pltpu.VMEM(o.shape, F32) for o in...  90.4 us
    unnamed x3, local copies, waits for them, and re-layouts  3.1 us

profile of v6, /device:TPU:0, one launch (start us, length us, event | category | flops | bytes accessed | tf_op | source)
XLA Modules:
  0.0 94.1 jit_solution(9253695044466889708)
XLA Ops:
  0.6 90.4 %quantizer_step.1 = (f32[3,64,768]{2,1,0:T(8,128)S(1)}, f32[2,4,4,24,768]{4,3,2,1,0:T(8,128)S(1)}, f32[256,768]{1,0:T(8,128)S(1)}) custom-call(bf16[256,768]{1,0:T(8,128)(2,1)} %hid_hbm.1, bf16[768,768]{1,0:T(8,128)(2,1)} %w_hbm.1, bf16[3,2048,768]{2,1,0:T(8,128)(2,1)} %cb_hbm.1, s32[3,256]{1,0:T(4,128)} %codes.1), custom_call_target="tpu_custom_call" | custom-call | flops 12999999488 | bytes 16000000 | tf_op jit(solution)/shard_map/quantizer_step/pallas_call | solution.py:556
  91.0 0.8 copy.11
  91.9 1.4 %copy.12 = f32[768,768]{1,0:T(8,128)} copy(f32[768,768]{1,0:T(8,128)S(1)} %bitcast.4) | data formatting | bytes 4718592
  93.3 0.9 copy.13
